TPU v7x, 32 devices: a whole 2x2x4 slice. The times are simulated.
32 devices in a mesh: ctx: 4 (over z), section: 2 (over x), dp: 4 (over y, core).
Axes of the slice: x: 2, y: 2, z: 4, core: 2. Of those that a mesh axis runs over, the one named last changes fastest.
Arguments:
- query_vectors: bfloat16 [4, 512, 1792], P('dp', 'ctx', 'section'), may hold values from -16 to 16
- key_vectors: bfloat16 [4, 512, 256], P('dp', 'ctx', 'section'), may hold values from -16 to 16
- value_vectors: bfloat16 [4, 512, 256], P('dp', 'ctx', 'section'), may hold values from -6 to 6
- grad_output: bfloat16 [4, 512, 1792], P('dp', 'ctx', 'section'), may hold values from -24 to 24
- output_dots: float32 [4, 14, 512], P('dp', 'section', 'ctx'), may hold values from -12 to 12
- frame_ids: int32 [4, 512], P('dp'), may hold values from 0 to 3, never falling along the last dimension, each value on 1 to 256 neighbouring positions
- visual_rows: int32 [4, 4, 32], P('dp', 'ctx'), may hold values from 0 to 127, as said below
- shuffle_source: int32 [4, 8, 64], P('dp', ('ctx', 'section')), may hold values from 0 to 63, each once within a row
- qkv_weight: bfloat16 [2304, 3584], P(None, ('section', 'dp')), may hold values from -0.125 to 0.125
- projector_weight: bfloat16 [3584, 2560], P(('section', 'dp')), may hold values from -0.09375 to 0.09375
Outputs:
- grad_keys: bfloat16 [4, 512, 256], P('dp', 'ctx', 'section')
- grad_values: bfloat16 [4, 512, 256], P('dp', 'ctx', 'section')
- patch_grads: bfloat16 [4, 512, 640], P('dp', ('ctx', 'section'))
Inputs may be any that keep to these rules, and one draw needn't show every extreme that they name: `frame_ids`: frame numbers never fall along a sequence; a frame holds 1 to 256 tokens. `visual_rows`: each block of 128 tokens lists 32 distinct positions in increasing order. `shuffle_source`: each row is a permutation.
All inputs are finite; a program needn't handle non-finite values.
Results may differ from a plain program's by a relative error of at most 0.014.
Values may be sent and summed in bfloat16 or wider, within the bound.
A program may use at most 128 MiB of HBM per device.

v0:
```python
import math

import jax
import jax.numpy as jnp
from jax import lax
from jax.sharding import PartitionSpec as P

HEAD_DIM = 128
GROUP = 7


MASKED = -1e30


def shifted(value, axis, steps):
    count = lax.axis_size(axis)
    pairs = [(source, (source + steps) % count) for source in range(count)]
    return lax.ppermute(value, axis, pairs)


def shards(
    query_vectors,
    key_vectors,
    value_vectors,
    grad_output,
    output_dots,
    frame_ids,
    visual_rows,
    shuffle_source,
    qkv_weight,
    projector_weight,
):
    loop_size = lax.axis_size("ctx")
    position = lax.axis_index("ctx")
    local_rows = query_vectors.shape[1]
    scale_factor = 1.0 / math.sqrt(HEAD_DIM)
    query_heads = query_vectors[0].reshape(local_rows, GROUP, HEAD_DIM)
    grad_heads = grad_output[0].reshape(local_rows, GROUP, HEAD_DIM)
    corrections = output_dots[0]
    frame_line = frame_ids[0]
    query_first = position * local_rows
    query_pos = query_first + jnp.arange(local_rows, dtype=jnp.int32)
    query_frames = lax.dynamic_slice_in_dim(frame_line, query_first, local_rows)
    last_frame = query_frames[local_rows - 1]
    own_pair = jnp.stack([key_vectors[0], value_vectors[0]])

    def key_mask(key_first, row_count):
        key_pos = key_first + jnp.arange(row_count, dtype=jnp.int32)
        key_frames = lax.dynamic_slice_in_dim(frame_line, key_first, row_count)
        allowed = (key_pos[None, :] <= query_pos[:, None]) | (
            key_frames[None, :] == query_frames[:, None]
        )
        return (allowed, key_frames[0] <= last_frame)

    def scores_for(key_block):
        return (
            jnp.einsum("qhd,kd->hqk", query_heads, key_block, preferred_element_type=jnp.float32)
            * scale_factor
        )

    start_pair = (
        jnp.full((GROUP, local_rows), MASKED, jnp.float32),
        jnp.zeros((GROUP, local_rows), jnp.float32),
    )
    key_block = lax.all_gather(key_vectors, "ctx", axis=1, tiled=True)[0]
    allowed, needed = key_mask(jnp.int32(0), key_block.shape[0])

    def update(pair_state):
        running, summed = pair_state
        scores = jnp.where(allowed[None], scores_for(key_block), MASKED)
        newest = jnp.maximum(running, scores.max(axis=-1))
        summed = jnp.exp(scores - newest[:, :, None]).sum(axis=-1)
        return (newest, summed)

    running, summed = lax.cond(needed, update, lambda unchanged: unchanged, start_pair)
    log_total = running + jnp.log(summed)

    def process(pair_block, grads_block, grad_query, block_index):
        allowed, needed = key_mask(block_index * local_rows, local_rows)

        def compute(state_now):
            grads_now, query_now = state_now
            key_block = pair_block[0]
            value_block = pair_block[1]
            probability = jnp.exp(
                jnp.where(allowed[None], scores_for(key_block) - log_total[:, :, None], MASKED)
            )
            probs_low = probability.astype(jnp.bfloat16)
            grad_probs = jnp.einsum(
                "qhd,kd->hqk", grad_heads, value_block, preferred_element_type=jnp.float32
            )
            grad_scores = (probability * (grad_probs - corrections[:, :, None])).astype(
                jnp.bfloat16
            )
            query_now = (
                query_now
                + jnp.einsum(
                    "hqk,kd->qhd", grad_scores, key_block, preferred_element_type=jnp.float32
                )
                * scale_factor
            )
            key_term = (
                jnp.einsum(
                    "hqk,qhd->kd", grad_scores, query_heads, preferred_element_type=jnp.float32
                )
                * scale_factor
            )
            value_term = jnp.einsum(
                "hqk,qhd->kd", probs_low, grad_heads, preferred_element_type=jnp.float32
            )
            return (grads_now + jnp.stack([key_term, value_term]), query_now)

        return lax.cond(needed, compute, lambda unchanged: unchanged, (grads_block, grad_query))

    def move_keys(pair_block, offset):
        return shifted(pair_block, "ctx", offset)

    def move_grads(grads_block, offset):
        return shifted(grads_block, "ctx", offset)

    zero_grads = jnp.zeros((2, local_rows, HEAD_DIM), jnp.float32)
    zero_query = jnp.zeros((local_rows, GROUP, HEAD_DIM), jnp.float32)

    def one_turn(turn_index, state_now):
        pair_block, grads_block, query_now = state_now
        grads_block, query_now = process(
            pair_block, grads_block, query_now, (position - turn_index) % loop_size
        )
        return (move_keys(pair_block, 1), move_grads(grads_block, 1), query_now)

    carried = (own_pair, zero_grads, zero_query)
    rounds = loop_size // 4

    def four_turns(round_index, state_now):
        for within in range(4):
            state_now = one_turn(round_index * 4 + within, state_now)
        return state_now

    carried = lax.fori_loop(0, rounds, four_turns, carried)
    final_pair, summed_grads, grad_query = carried
    grad_keys_low = summed_grads[0].astype(jnp.bfloat16)
    grad_values_low = summed_grads[1].astype(jnp.bfloat16)
    grad_query_low = grad_query.astype(jnp.bfloat16).reshape(local_rows, GROUP * HEAD_DIM)
    visual_picks = visual_rows[0, 0]
    chosen = jnp.concatenate(
        [grad_query_low[visual_picks], grad_keys_low[visual_picks], grad_values_low[visual_picks]],
        axis=1,
    )
    everyone = lax.all_gather(chosen[None], ("section", "dp"), axis=0, tiled=True)
    groups = lax.axis_size("section")
    replicas = lax.axis_size("dp")
    half_rows = visual_picks.shape[0] // 2
    width_in = chosen.shape[1]
    arranged = (
        everyone.reshape(groups, replicas, 2, half_rows, width_in)
        .transpose(2, 1, 3, 0, 4)
        .reshape(2 * replicas * half_rows, groups * width_in)
    )
    visual_grad = jnp.dot(arranged, qkv_weight, preferred_element_type=jnp.float32).astype(
        jnp.bfloat16
    )
    shuffled = lax.psum_scatter(
        jnp.dot(visual_grad, projector_weight, preferred_element_type=jnp.float32).astype(
            jnp.bfloat16
        ),
        ("section", "dp"),
        scatter_dimension=0,
        tiled=True,
    ).astype(jnp.float32)
    slot_rows = shuffled.reshape(half_rows * 4, projector_weight.shape[1] // 4)
    patches = slot_rows[shuffle_source[0, 0]].astype(jnp.bfloat16)
    return (grad_keys_low[None], grad_values_low[None], patches[None])


def solution(mesh):
    placed = (
        P("dp", "ctx", "section"),
        P("dp", "ctx", "section"),
        P("dp", "ctx", "section"),
        P("dp", "ctx", "section"),
        P("dp", "section", "ctx"),
        P("dp", None),
        P("dp", "ctx", None),
        P("dp", ("ctx", "section"), None),
        P(None, ("section", "dp")),
        P(("section", "dp"), None),
    )
    return jax.shard_map(
        shards,
        mesh=mesh,
        in_specs=placed,
        out_specs=(
            P("dp", "ctx", "section"),
            P("dp", "ctx", "section"),
            P("dp", ("ctx", "section"), None),
        ),
        check_vma=False,
    )
```

profile of v0, /device:TPU:0, one launch (start us, length us, event | category | flops | bytes accessed | tf_op | source)
XLA Modules:
  0.0 140.3 jit_solution(6935848132442366423)
XLA Ops:
  7.3 15.4 %all_gather.6 = bf16[1,512,128]{2,1,0:T(8,128)(2,1)S(1)} all-gather(bf16[1,128,128]{2,1,0:T(8,128)(2,1)} %param.21), channel_id=1, replica_groups=mesh['ctx'=4,'section'=2,'dp'=4] {'ctx'}, dimensions={1}, use_global_device_ids=true | all-gather | bytes 163840 | tf_op jit(solution)/shard_map/all_gather | solution.py:65
  22.7 1.4 constant_dynamic-update-slice_fusion.1
  24.1 1.1 copy.30
  25.2 1.2 slice.63
  29.0 1.1 copy.32
  30.9 2.9 %conditional.5 = (f32[7,128]{1,0:T(8,128)}, f32[7,128]{1,0:T(8,128)S(1)}) conditional(s32[]{:T(128)} %bitcast.69, () %tuple.59, (s32[128]{0:T(128)S(1)}, s32[128,512]{0,1:T(8,128)S(1)}, s32[1,512]{1,0:T(1,128)}, s32[128]{0:T(128)S(1)}, bf16[1,512,128]{2,1,0:T(8,128)(2,1)S(1)}, /*index=5*/bf16[128,7,128]{0,2,1:T(8,128)(2,1)S(1)}) %tuple.121), branch_computations={%region_0.0_spmd, %region_1.4_spmd} | conditional | flops 120847488 | bytes 4517392 | solution.py:75
  30.9 0.8 compare_or_fusion
  32.7 1.1 exponential_reduce_fusion
  35.2 3.7 %conditional.6 = ((f32[2,128,128]{2,1,0:T(8,128)S(1)}, f32[128,7,128]{2,0,1:T(8,128)S(1)})) conditional(s32[]{:T(128)} %bitcast.66, (f32[2,128,128]{2,1,0:T(8,128)S(1)}, f32[128,7,128]{2,0,1:T(8,128)S(1)}) %tuple.58, (s32[]{:T(128)}, s32[1,128]{1,0:T(1,128)S(1)}, s32[128,128]{0,1:T(8,128)S(1)}, s32[1,128]{1,0:T(1,128)S(1)}, s32[128,128]{0,1:T(8,128)S(1)}, ...), branch_computations={%region_4.5_spmd, %region_5.6_spmd} | conditional | flops 147964032 | bytes 4702236 | solution.py:113
  35.4 1.0 fusion.8
  36.4 1.0 fusion.11
  37.9 1.0 fusion.10
  38.9 1.9 %collective-permute-start = (f32[2,128,128]{2,1,0:T(8,128)S(1)}, f32[2,128,128]{2,1,0:T(8,128)}, u32[]{:S(2)}, u32[]{:S(2)}) collective-permute-start(f32[2,128,128]{2,1,0:T(8,128)S(1)} %get-tuple-element.290), channel_id=1, source_target_pairs={{0,8},{8,16},{16,24},{24,0},{1,9},{9,17},{17,25},{25,1},{2,10},{10... | collective-permute-start | bytes 393224 | tf_op jit(solution)/shard_map/while/body/eval_jaxpr/ppermute | solution.py:18
  41.6 4.3 %collective-permute-done = f32[2,128,128]{2,1,0:T(8,128)} collective-permute-done((f32[2,128,128]{2,1,0:T(8,128)S(1)}, f32[2,128,128]{2,1,0:T(8,128)}, u32[]{:S(2)}, u32[]{:S(2)}) %collective-permute-start) | collective-permute-done | bytes 131104 | tf_op jit(solution)/shard_map/while/body/eval_jaxpr/ppermute | solution.py:18
  45.9 1.4 collective-permute-done.1
  47.2 4.7 %collective-permute-start.2 = (f32[2,128,128]{2,1,0:T(8,128)}, f32[2,128,128]{2,1,0:T(8,128)}, u32[]{:S(2)}, u32[]{:S(2)}) collective-permute-start(f32[2,128,128]{2,1,0:T(8,128)} %get-tuple-element.292), channel_id=1, source_target_pairs={{0,8},{8,16},{16,24},{24,0},{1,9},{9,17},{17,25},{25,1},{2,10},{10... | collective-permute-start | bytes 393224 | tf_op jit(solution)/shard_map/while/body/eval_jaxpr/ppermute | solution.py:18
  51.9 1.8 %collective-permute-start.3 = (bf16[2,128,128]{2,1,0:T(8,128)(2,1)}, bf16[2,128,128]{2,1,0:T(8,128)(2,1)}, u32[]{:S(2)}, u32[]{:S(2)}) collective-permute-start(bf16[2,128,128]{2,1,0:T(8,128)(2,1)} %collective-permute-done.1), channel_id=1, source_target_pairs={{0,8},{8,16},{16,24},{24,0},{1,9},{9,17},{17,25},{25,1},{2,10},{10... | collective-permute-start | bytes 196616 | tf_op jit(solution)/shard_map/while/body/eval_jaxpr/ppermute | solution.py:18
  54.3 4.1 %collective-permute-done.3 = bf16[2,128,128]{2,1,0:T(8,128)(2,1)} collective-permute-done((bf16[2,128,128]{2,1,0:T(8,128)(2,1)}, bf16[2,128,128]{2,1,0:T(8,128)(2,1)}, u32[]{:S(2)}, u32[]{:S(2)}) %collective-permute-start.3) | collective-permute-done | bytes 65568 | tf_op jit(solution)/shard_map/while/body/eval_jaxpr/ppermute | solution.py:18
  58.4 1.3 collective-permute-start.5
  61.0 9.7 %collective-permute-done.4 = f32[2,128,128]{2,1,0:T(8,128)} collective-permute-done((f32[2,128,128]{2,1,0:T(8,128)}, f32[2,128,128]{2,1,0:T(8,128)}, u32[]{:S(2)}, u32[]{:S(2)}) %collective-permute-start.4) | collective-permute-done | bytes 131104 | tf_op jit(solution)/shard_map/while/body/eval_jaxpr/ppermute | solution.py:18
  70.8 5.6 %conditional.9 = (f32[2,128,128]{2,1,0:T(8,128)}, bf16[128,896]{1,0:T(8,128)(2,1)S(1)}) conditional(s32[]{:T(128)} %bitcast.63, (f32[2,128,128]{2,1,0:T(8,128)}, f32[128,7,128]{2,0,1:T(8,128)S(1)}) %tuple.66, (s32[]{:T(128)}, s32[1,128]{1,0:T(1,128)S(1)}, s32[128,128]{0,1:T(8,128)S(1)}, s32[1,128]{1,0:T(1,128)S(1)}, s32[128,128]{0,1:T(8,128)S(1)}, ...), branch_computations={%region_10.11_spmd, %region_11.12_spmd} | conditional | flops 148078720 | bytes 5849108 | solution.py:113
  70.9 1.0 fusion.62
  71.9 1.0 fusion.66
  73.4 1.6 %maximum_add_fusion.3 = f32[2,128,128]{2,1,0:T(8,128)} fusion(f32[2,128,128]{2,1,0:T(8,128)} %get-tuple-element.263, f32[1,128,128]{2,1,0:T(8,128)S(1)} %convolution_bitcast_fusion.10, f32[1,128,128]{2,1,0:T(8,128)S(1)} %fusion.68), kind=kLoop, calls=%fused_computation.110 | loop fusion | flops 65536 | bytes 393216 | tf_op jit(solution)/shard_map/while/body/eval_jaxpr/cond/branch_1_fun/add | solution.py:111
  75.1 1.0 fusion.65
  76.3 0.9 convert.10
  78.0 5.4 %collective-permute-done.6 = bf16[2,128,128]{2,1,0:T(8,128)(2,1)S(1)} collective-permute-done((bf16[2,128,128]{2,1,0:T(8,128)(2,1)S(1)}, bf16[2,128,128]{2,1,0:T(8,128)(2,1)S(1)}, u32[]{:S(2)}, u32[]{:S(2)}) %collective-permute-start.6) | collective-permute-done | bytes 65568 | tf_op jit(solution)/shard_map/while/body/eval_jaxpr/ppermute | solution.py:18
  84.6 10.0 %all-gather = bf16[256,1152]{1,0:T(8,128)(2,1)S(1)} all-gather(bf16[32,1152]{1,0:T(8,128)(2,1)S(1)} %pad_maximum_fusion), channel_id=2, replica_groups=mesh['ctx'=4,'section'=2,'dp'=4] {'section','dp'}, dimensions={0}, use_global_device_ids=true | all-gather | bytes 663552 | tf_op jit(solution)/shard_map/all_gather | solution.py:149
  95.3 3.8 %convolution_convert_fusion = bf16[128,2560]{1,0:T(8,128)(2,1)} fusion(bf16[448,2560]{1,0:T(8,128)(2,1)S(1)} %copy-done, bf16[128,2304]{1,0:T(8,128)(2,1)S(1)} %bitcast.276, bf16[2304,448]{0,1:T(8,128)(2,1)} %param.28), kind=kOutput, calls=%fused_computation.120 | convolution fusion | flops 558227456 | bytes 5603328 | tf_op jit(solution)/shard_map/dot_general | solution.py:163
  99.2 32.0 %reduce-scatter.2.cloned.1.call-done = bf16[16,2560]{1,0:T(8,128)(2,1)} async-done(((bf16[128,2560]{1,0:T(8,128)(2,1)}), bf16[16,2560]{1,0:T(8,128)(2,1)}) %reduce-scatter.2.cloned.1.call-update) | async-done | bytes 81936 | tf_op jit(solution)/shard_map/reduce_scatter | solution.py:162
  131.1 0.9 reshape.168
  132.1 1.3 gather_fusion.3
  (64 shorter events, 8.7 us)
Async XLA Ops:
  7.2 88.1 %copy-start = (bf16[448,2560]{1,0:T(8,128)(2,1)S(1)}, bf16[448,2560]{1,0:T(8,128)(2,1)}, u32[]{:S(2)}) copy-start(bf16[448,2560]{1,0:T(8,128)(2,1)} %param.29) | copy-start | bytes 6881284
  7.2 124.0 %reduce-scatter.2.cloned.1.call-start = ((), (), s32[]{:S(2)}) async-start(), calls=%async_computation.1 | async-start | bytes 737280 | tf_op jit(solution)/shard_map/reduce_scatter | solution.py:162
  30.8 3.7 %copy-start.4 = (bf16[1,128,128]{2,1,0:T(8,128)(2,1)S(1)}, bf16[1,128,128]{2,1,0:T(8,128)(2,1)}, u32[]{:S(2)}) copy-start(bf16[1,128,128]{2,1,0:T(8,128)(2,1)} %param.22) | copy-start | bytes 98308
  30.8 4.4 %copy-start.3 = (f32[1,7,128]{2,0,1:T(1,128)S(1)}, f32[1,7,128]{2,0,1:T(1,128)}, u32[]{:S(2)}) copy-start(f32[1,7,128]{2,0,1:T(1,128)} %param.24) | copy-start | bytes 10756
  38.9 6.9 %collective-permute-start = (f32[2,128,128]{2,1,0:T(8,128)S(1)}, f32[2,128,128]{2,1,0:T(8,128)}, u32[]{:S(2)}, u32[]{:S(2)}) collective-permute-start(f32[2,128,128]{2,1,0:T(8,128)S(1)} %get-tuple-element.290), channel_id=1, source_target_pairs={{0,8},{8,16},{16,24},{24,0},{1,9},{9,17},{17,25},{25,1},{2,10},{10... | collective-permute-start | bytes 393224 | tf_op jit(solution)/shard_map/while/body/eval_jaxpr/ppermute | solution.py:18
  40.8 6.4 %collective-permute-start.1 = (bf16[2,128,128]{2,1,0:T(8,128)(2,1)}, bf16[2,128,128]{2,1,0:T(8,128)(2,1)}, u32[]{:S(2)}, u32[]{:S(2)}) collective-permute-start(bf16[2,128,128]{2,1,0:T(8,128)(2,1)} %constant_dynamic-update-slice_fusion), channel_id=1, source_target_pairs={{0,8},{8,16},{16,24},{24,0},{1,9},{9,17},{17,25},{25,1},{2,10},{10... | collective-permute-start | bytes 196616 | tf_op jit(solution)/shard_map/while/body/eval_jaxpr/ppermute | solution.py:18
  47.2 12.5 %collective-permute-start.2 = (f32[2,128,128]{2,1,0:T(8,128)}, f32[2,128,128]{2,1,0:T(8,128)}, u32[]{:S(2)}, u32[]{:S(2)}) collective-permute-start(f32[2,128,128]{2,1,0:T(8,128)} %get-tuple-element.292), channel_id=1, source_target_pairs={{0,8},{8,16},{16,24},{24,0},{1,9},{9,17},{17,25},{25,1},{2,10},{10... | collective-permute-start | bytes 393224 | tf_op jit(solution)/shard_map/while/body/eval_jaxpr/ppermute | solution.py:18
  51.9 6.5 %collective-permute-start.3 = (bf16[2,128,128]{2,1,0:T(8,128)(2,1)}, bf16[2,128,128]{2,1,0:T(8,128)(2,1)}, u32[]{:S(2)}, u32[]{:S(2)}) collective-permute-start(bf16[2,128,128]{2,1,0:T(8,128)(2,1)} %collective-permute-done.1), channel_id=1, source_target_pairs={{0,8},{8,16},{16,24},{24,0},{1,9},{9,17},{17,25},{25,1},{2,10},{10... | collective-permute-start | bytes 196616 | tf_op jit(solution)/shard_map/while/body/eval_jaxpr/ppermute | solution.py:18
  58.4 12.4 %collective-permute-start.5 = (bf16[2,128,128]{2,1,0:T(8,128)(2,1)}, bf16[2,128,128]{2,1,0:T(8,128)(2,1)}, u32[]{:S(2)}, u32[]{:S(2)}) collective-permute-start(bf16[2,128,128]{2,1,0:T(8,128)(2,1)} %collective-permute-done.3), channel_id=1, source_target_pairs={{0,8},{8,16},{16,24},{24,0},{1,9},{9,17},{17,25},{25,1},{2,10},{10... | collective-permute-start | bytes 196616 | tf_op jit(solution)/shard_map/while/body/eval_jaxpr/ppermute | solution.py:18
  59.7 0.7 copy-start.5
  59.7 11.1 %collective-permute-start.4 = (f32[2,128,128]{2,1,0:T(8,128)}, f32[2,128,128]{2,1,0:T(8,128)}, u32[]{:S(2)}, u32[]{:S(2)}) collective-permute-start(f32[2,128,128]{2,1,0:T(8,128)} %get-tuple-element.294), channel_id=1, source_target_pairs={{0,8},{8,16},{16,24},{24,0},{1,9},{9,17},{17,25},{25,1},{2,10},{10... | collective-permute-start | bytes 393224 | tf_op jit(solution)/shard_map/while/body/eval_jaxpr/ppermute | solution.py:18
  77.3 6.1 %collective-permute-start.6 = (bf16[2,128,128]{2,1,0:T(8,128)(2,1)S(1)}, bf16[2,128,128]{2,1,0:T(8,128)(2,1)S(1)}, u32[]{:S(2)}, u32[]{:S(2)}) collective-permute-start(bf16[2,128,128]{2,1,0:T(8,128)(2,1)S(1)} %convert.10), channel_id=1, source_target_pairs={{0,8},{8,16},{16,24},{24,0},{1,9},{9,17},{17,25},{25,1},{2,10},{10... | collective-permute-start | bytes 196616 | tf_op jit(solution)/shard_map/while/body/eval_jaxpr/ppermute | solution.py:18
  83.4 15.7 %copy-start.1 = (bf16[1,128,128]{2,1,0:T(8,128)(2,1)}, bf16[1,128,128]{2,1,0:T(8,128)(2,1)S(1)}, u32[]{:S(2)}) copy-start(bf16[1,128,128]{2,1,0:T(8,128)(2,1)S(1)} %get-tuple-element.410) | copy-start | bytes 98308
  83.4 15.7 %copy-start.2 = (bf16[1,128,128]{2,1,0:T(8,128)(2,1)}, bf16[1,128,128]{2,1,0:T(8,128)(2,1)S(1)}, u32[]{:S(2)}) copy-start(bf16[1,128,128]{2,1,0:T(8,128)(2,1)S(1)} %get-tuple-element.411) | copy-start | bytes 98308
  95.3 3.8 %copy-start.6 = (s32[1,1,64]{2,1,0:T(1,128)S(1)}, s32[1,1,64]{2,1,0:T(1,128)}, u32[]{:S(2)}) copy-start(s32[1,1,64]{2,1,0:T(1,128)} %param.27) | copy-start | bytes 772
Sparse Core Ops, SparseCore 0:
  99.2 31.8 reduce-scatter.1
where the time goes:
time: 142 us; the launch traced here: 140 us
  waiting for transfers between devices  56.9 us (40%)
  blocking collectives  25.4 us (18%)
  between operations  18.3 us (13%)
  local copies, waits for them, and re-layouts  12.6 us (9%)
  matrix products  11.1 us (8%)
  starting transfers between devices  9.85 us (7%)
  other arithmetic  5.95 us (4%)
    reduce_scatter x1, waiting for transfers between devices, shards(): lax.psum_scatter(jnp.dot(visual_grad, projector_weight, preferred_element...  32 us
    ppermute x7, waiting for transfers between devices, shifted(): return lax.ppermute(value, axis, pairs)  24.9 us
    all_gather x1, blocking collectives, shards(): key_block = lax.all_gather(key_vectors, 'ctx', axis=1, tiled=True)[0]  15.4 us
    all_gather x1, blocking collectives, shards(): lax.all_gather(chosen[None], ('section', 'dp'), axis=0, tiled=True)  10 us
    ppermute x7, starting transfers between devices, shifted(): return lax.ppermute(value, axis, pairs)  9.82 us
    unnamed x18, local copies, waits for them, and re-layouts  4.25 us
    dot_general x1, matrix products, shards(): jnp.dot(visual_grad, projector_weight, preferred_element_type=jnp.float32)  3.77 us
  transfers between devices with their start and end apart: 8, of which 6 were waited for; matrix products, arithmetic and copies ran while one was open for 0% of the time, Pallas kernels for 0%

commit v1 on v0

v1 whole, which is shorter than its diff:
```python
import functools
import math

import jax
import jax.numpy as jnp
from jax import lax
from jax.experimental import pallas as pl
from jax.experimental.pallas import tpu as pltpu
from jax.sharding import PartitionSpec as P

HEAD = 128
GROUP = 7
MASKED = -1e30
MESH = pl.DeviceIdType.MESH
CHUNKS = 2
BF = jnp.bfloat16
F32 = jnp.float32


def dot(a, b, over=(1, 0)):
    return lax.dot_general(a, b, (((over[0],), (over[1],)), ((), ())), preferred_element_type=F32)


def kernel(
    n, sections, replicas,
    q_in, k_in, v_in, g_in, dots, frames, rows, source, wq_in, wp_in,
    dk_out, dv_out, patch_out,
    qs, gs, kbuf, vbuf, sbuf, gsend, grecv, wq, wp, top, total, gq_acc, gqsel, kvsel, psend, precv,
    load_sem, k_send, k_recv, v_send, v_recv, g_send, g_recv, a_send, a_recv, b_send, b_recv, p_send, p_recv,
):
    me = lax.axis_index("ctx")
    sec = lax.axis_index("section")
    rep = lax.axis_index("dp")
    tok = k_in.shape[1]
    vis = rows.shape[2]
    half = vis // 2
    width = GROUP * HEAD
    scale = 1.0 / math.sqrt(HEAD)
    factor = scale * math.log2(math.e)
    plane = [(a, b) for a in range(sections) for b in range(replicas) if a or b]

    def each(low, high, body):
        if n <= 8:
            for at in range(low, high):
                body(at)
        else:
            lax.fori_loop(low, high, lambda at, c: (body(at), c)[1], 0)

    def ahead(o):
        return {"ctx": lax.rem(me + o, n)}

    def behind(o):
        return {"ctx": lax.rem(me - o + n, n)}

    def peer(a, b):
        return {"section": lax.rem(sec + a, sections), "dp": lax.rem(rep + b, replicas)}

    def peer_back(a, b):
        return {"section": lax.rem(sec + a, sections), "dp": lax.rem(rep - b + replicas, replicas)}

    barrier = pltpu.get_barrier_semaphore()
    each(1, n, lambda o: pl.semaphore_signal(barrier, inc=1, device_id=ahead(o), device_id_type=MESH))
    for a, b in plane:
        pl.semaphore_signal(barrier, inc=1, device_id=peer(a, b), device_id_type=MESH)

    loads = [
        pltpu.make_async_copy(k_in.at[0], kbuf.at[0], load_sem.at[0]),
        pltpu.make_async_copy(v_in.at[0], vbuf.at[0], load_sem.at[1]),
        pltpu.make_async_copy(wq_in, wq, load_sem.at[2]),
        pltpu.make_async_copy(wp_in, wp, load_sem.at[3]),
    ]
    q_loads = [
        pltpu.make_async_copy(
            q_in.at[0, :, pl.ds(h * HEAD, HEAD)], qs.at[pl.ds(h * HEAD, HEAD), :], load_sem.at[4 + h]
        )
        for h in range(GROUP)
    ]
    g_loads = [
        pltpu.make_async_copy(
            g_in.at[0, :, pl.ds(h * HEAD, HEAD)], gs.at[pl.ds(h * HEAD, HEAD), :], load_sem.at[4 + GROUP + h]
        )
        for h in range(GROUP)
    ]
    loads[0].start()
    for c in q_loads:
        c.start()
    loads[1].start()
    for c in g_loads:
        c.start()
    loads[2].start()
    loads[3].start()
    pl.semaphore_wait(barrier, (n - 1) + len(plane))

    def remote(src, dst, send, recv, device):
        return pltpu.make_async_remote_copy(
            src_ref=src, dst_ref=dst, send_sem=send, recv_sem=recv, device_id=device, device_id_type=MESH
        )

    def k_copy(o):
        return remote(k_in.at[0], kbuf.at[o], k_send.at[o], k_recv.at[o], ahead(o))

    def v_copy(o):
        return remote(v_in.at[0], vbuf.at[o], v_send.at[o], v_recv.at[o], ahead(o))

    def g_copy(o):
        return remote(gsend.at[o], grecv.at[o], g_send.at[o], g_recv.at[o], behind(o))

    def sel_copy(buf, send, recv, a, b):
        return remote(
            buf.at[0, pl.ds(0, vis)], buf.at[a, pl.ds(b * vis, vis)], send.at[a, b], recv.at[a, b], peer(a, b)
        )

    columns = wp.shape[1] // CHUNKS

    def p_copy(i, a, b):
        first = b * vis + lax.rem(sec + a, sections) * half
        return remote(
            psend.at[i, pl.ds(pl.multiple_of(first, half), half)],
            precv.at[i, a, b],
            p_send.at[i, a, b],
            p_recv.at[i, a, b],
            peer_back(a, b),
        )

    each(1, n, lambda o: k_copy(o).start())
    each(1, n, lambda o: v_copy(o).start())

    query_frames = frames[:, pl.ds(pl.multiple_of(me * tok, tok), tok)]
    row_at = lax.broadcasted_iota(jnp.int32, (tok, tok), 0)
    col_at = lax.broadcasted_iota(jnp.int32, (tok, tok), 1)
    hot_t = (lax.broadcasted_iota(jnp.int32, (tok, vis), 0) == rows[0]).astype(F32).astype(BF)
    eye = (row_at == col_at).astype(F32).astype(BF)
    hot = dot(hot_t, eye, (0, 0)).astype(BF)
    dots_row = jnp.concatenate([dots[0, h : h + 1, :] for h in range(GROUP)], axis=1)

    def bias_for(o):
        first = lax.rem(me - o + n, n) * tok
        line = frames[:, pl.ds(pl.multiple_of(first, tok), tok)].astype(F32)
        key_frames = jnp.transpose(jnp.broadcast_to(line, (tok, tok)))
        allowed = (first + row_at <= me * tok + col_at) | (key_frames == query_frames.astype(F32))
        bias = jnp.where(allowed, 0.0, MASKED)
        return jnp.concatenate([bias] * GROUP, axis=1)

    top[...] = jnp.full_like(top, MASKED)
    total[...] = jnp.zeros_like(total)
    gq_acc[...] = jnp.zeros_like(gq_acc)

    def first_pass(o):
        s = dot(kbuf[o], qs[...], (1, 1)) + bias_for(o)
        sbuf[o] = s
        top[...] = jnp.maximum(top[...], jnp.max(s, axis=0, keepdims=True))

    def first_remote(o):
        k_copy(o).wait_recv()
        first_pass(o)

    loads[0].wait()
    for c in q_loads:
        c.wait()
    first_pass(0)
    each(1, n, first_remote)

    def second_pass(o):
        e = jnp.exp2((sbuf[o] - top[...]) * factor)
        sbuf[o] = e
        total[...] += jnp.sum(e, axis=0, keepdims=True)

    each(0, n, second_pass)
    total[...] = 1.0 / total[...]

    loads[1].wait()
    for c in g_loads:
        c.wait()

    def third_pass(o):
        p = sbuf[o] * total[...]
        gp = dot(vbuf[o], gs[...], (1, 1))
        gsc = (p * (gp - dots_row)).astype(BF)
        gv = dot(p.astype(BF), gs[...])
        gk = dot(gsc, qs[...]) * scale
        gq_acc[...] += dot(kbuf[o], gsc, (0, 0))
        return gk, gv

    def third_remote(o):
        v_copy(o).wait_recv()
        gk, gv = third_pass(o)
        gsend[o, 0] = gk.astype(BF)
        gsend[o, 1] = gv.astype(BF)
        g_copy(o).start()

    each(1, n, third_remote)
    gk, gv = third_pass(0)

    gq = (gq_acc[...] * scale).astype(BF)
    for h in range(GROUP):
        gqsel[0, 0:vis, h * HEAD : (h + 1) * HEAD] = dot(
            hot, gq[:, h * HEAD : (h + 1) * HEAD], (1, 1)
        ).astype(BF)
    for a, b in plane:
        sel_copy(gqsel, a_send, a_recv, a, b).start()

    if n <= 8:
        for o in range(1, n):
            g_copy(o).wait_recv()
            gk = gk + grecv[o, 0].astype(F32)
            gv = gv + grecv[o, 1].astype(F32)
    else:

        def gather(o, pair):
            g_copy(o).wait_recv()
            return pair[0] + grecv[o, 0].astype(F32), pair[1] + grecv[o, 1].astype(F32)

        gk, gv = lax.fori_loop(1, n, gather, (gk, gv))
    gk, gv = gk.astype(BF), gv.astype(BF)
    kvsel[0, 0:vis, 0:HEAD] = dot(hot, gk).astype(BF)
    kvsel[0, 0:vis, HEAD : 2 * HEAD] = dot(hot, gv).astype(BF)
    for a, b in plane:
        sel_copy(kvsel, b_send, b_recv, a, b).start()
    dk_out[0] = gk
    dv_out[0] = gv

    loads[2].wait()
    loads[3].wait()
    part = width + 2 * HEAD
    for a, b in plane:
        sel_copy(gqsel, a_send, a_recv, a, b).wait_recv()

    def weight_rows(a, offset, size):
        first = lax.rem(sec - a + sections, sections) * part + offset
        return wq[pl.ds(pl.multiple_of(first, HEAD), size), :]

    grad = dot(gqsel[0], weight_rows(0, 0, width))
    for a in range(1, sections):
        grad = grad + dot(gqsel[a], weight_rows(a, 0, width))
    for a, b in plane:
        sel_copy(kvsel, b_send, b_recv, a, b).wait_recv()
    for a in range(sections):
        grad = grad + dot(kvsel[a], weight_rows(a, width, 2 * HEAD))
    grad = grad.astype(BF)

    for i in range(CHUNKS):
        psend[i] = dot(grad, wp[:, i * columns : (i + 1) * columns]).astype(BF)
        for a, b in plane:
            p_copy(i, a, b).start()

    slots = source.shape[2]
    quarter = wp.shape[1] // 4
    at = lax.broadcasted_iota(jnp.int32, (slots, slots), 0)
    slot_of = lax.rem(at, half) * 4 + lax.div(at, half)
    moved_t = (slot_of == source[0]).astype(F32).astype(BF)

    pieces = []
    for i in range(CHUNKS):
        mine = psend[i, pl.ds(pl.multiple_of(sec * half, half), half), :].astype(F32)
        for a, b in plane:
            p_copy(i, a, b).wait_recv()
            mine = mine + precv[i, a, b].astype(F32)
        for c in range(columns // quarter):
            pieces.append(mine[:, c * quarter : (c + 1) * quarter])
    merged = jnp.concatenate(pieces, axis=0).astype(BF)
    patch_out[0] = dot(moved_t, merged, (0, 0)).astype(BF)

    each(1, n, lambda o: k_copy(o).wait_send())
    each(1, n, lambda o: v_copy(o).wait_send())
    each(1, n, lambda o: g_copy(o).wait_send())
    for a, b in plane:
        sel_copy(gqsel, a_send, a_recv, a, b).wait_send()
        sel_copy(kvsel, b_send, b_recv, a, b).wait_send()
        for i in range(CHUNKS):
            p_copy(i, a, b).wait_send()


def solution(mesh):
    n, sections, replicas = mesh.shape["ctx"], mesh.shape["section"], mesh.shape["dp"]

    def shards(q, k, v, g, dots, frames, rows, source, wq, wp):
        tok, vis = k.shape[1], rows.shape[2]
        half = vis // 2
        width = GROUP * HEAD
        slots, quarter = source.shape[2], wp.shape[1] // 4
        anywhere = pl.BlockSpec(memory_space=pl.ANY)
        inside = pl.BlockSpec(memory_space=pltpu.VMEM)
        dma = pltpu.SemaphoreType.DMA
        return pl.pallas_call(
            functools.partial(kernel, n, sections, replicas),
            out_shape=(
                jax.ShapeDtypeStruct(k.shape, BF),
                jax.ShapeDtypeStruct(v.shape, BF),
                jax.ShapeDtypeStruct((1, slots, quarter), BF),
            ),
            in_specs=[anywhere] * 4 + [inside] * 4 + [anywhere] * 2,
            out_specs=(inside, inside, inside),
            scratch_shapes=[
                pltpu.VMEM((width, HEAD), BF),
                pltpu.VMEM((width, HEAD), BF),
                pltpu.VMEM((n, tok, HEAD), BF),
                pltpu.VMEM((n, tok, HEAD), BF),
                pltpu.VMEM((n, tok, width), F32),
                pltpu.VMEM((n, 2, tok, HEAD), BF),
                pltpu.VMEM((n, 2, tok, HEAD), BF),
                pltpu.VMEM(wq.shape, BF),
                pltpu.VMEM(wp.shape, BF),
                pltpu.VMEM((1, width), F32),
                pltpu.VMEM((1, width), F32),
                pltpu.VMEM((HEAD, width), F32),
                pltpu.VMEM((sections, replicas * vis, width), BF),
                pltpu.VMEM((sections, replicas * vis, 2 * HEAD), BF),
                pltpu.VMEM((CHUNKS, replicas * vis, wp.shape[1] // CHUNKS), BF),
                pltpu.VMEM((CHUNKS, sections, replicas, half, wp.shape[1] // CHUNKS), BF),
                dma((4 + 2 * GROUP,)),
                dma((n,)), dma((n,)), dma((n,)), dma((n,)), dma((n,)), dma((n,)),
                dma((sections, replicas)), dma((sections, replicas)),
                dma((sections, replicas)), dma((sections, replicas)),
                dma((CHUNKS, sections, replicas)), dma((CHUNKS, sections, replicas)),
            ],
            compiler_params=pltpu.CompilerParams(
                collective_id=0, has_side_effects=True, vmem_limit_bytes=56 * 1024 * 1024
            ),
        )(q, k, v, g, dots, frames, rows, source, wq, wp)

    placed = (
        P("dp", "ctx", "section"),
        P("dp", "ctx", "section"),
        P("dp", "ctx", "section"),
        P("dp", "ctx", "section"),
        P("dp", "section", "ctx"),
        P("dp", None),
        P("dp", "ctx", None),
        P("dp", ("ctx", "section"), None),
        P(None, ("section", "dp")),
        P(("section", "dp"), None),
    )
    return jax.shard_map(
        shards,
        mesh=mesh,
        in_specs=placed,
        out_specs=(
            P("dp", "ctx", "section"),
            P("dp", "ctx", "section"),
            P("dp", ("ctx", "section"), None),
        ),
        check_vma=False,
    )
```

time: 142 us -> 46 us (0.32)
  waiting for transfers between devices: 56.9 us -> 0 us
  Pallas kernels: 0 us -> 35.3 us
  blocking collectives: 25.4 us -> 0 us
  between operations: 18.3 us -> 0.64 us
  matrix products: 11.1 us -> 0 us
  starting transfers between devices: 9.85 us -> 0 us
  other arithmetic: 5.95 us -> 0 us
  local copies, waits for them, and re-layouts: 12.6 us -> 9.71 us
    pallas_call x0 -> x1, Pallas kernels: none -> 35.3 us  [shards(): pl.pallas_call(functools.partial(kernel, n, sections, replicas), out_shap...]
    reduce_scatter x1 -> x0, waiting for transfers between devices: 32 us -> none  [shards(): lax.psum_scatter(jnp.dot(visual_grad, projector_weight, preferred_element...]
    all_gather x2 -> x0, blocking collectives: 25.4 us -> none  [the longest x1 15.4 us: shards(): key_block = lax.all_gather(key_vectors, 'ctx', axis=1, tiled=True)[0]]
    ppermute x7 -> x0, waiting for transfers between devices: 24.9 us -> none  [shifted(): return lax.ppermute(value, axis, pairs)]
    dot_general x12 -> x0, matrix products: 11.1 us -> none  [the longest x1 3.77 us: shards(): jnp.dot(visual_grad, projector_weight, preferred_element_type=jnp.float32)]
    ppermute x7 -> x0, starting transfers between devices: 9.82 us -> none  [shifted(): return lax.ppermute(value, axis, pairs)]
    unnamed x18 -> x5, local copies, waits for them, and re-layouts: 4.25 us -> 9.71 us
    gather x4 -> x0, local copies, waits for them, and re-layouts: 3.17 us -> none  [the longest x1 1.34 us: shards(): patches = slot_rows[shuffle_source[0, 0]].astype(jnp.bfloat16)]
  transfers between devices with their start and end apart: 8 -> 0, of which waited for: 6 -> 0; matrix products, arithmetic and copies ran while one was open for 0% -> 0% of each run, Pallas kernels for 0% -> 0%
where the time goes in v1:
time: 46 us; the launch traced here: 45.6 us
  Pallas kernels  35.3 us (77%)
  local copies, waits for them, and re-layouts  9.71 us (21%)
  between operations  0.64 us (1%)
    pallas_call x1, Pallas kernels, shards(): pl.pallas_call(functools.partial(kernel, n, sections, replicas), out_shap...  35.3 us
    unnamed x5, local copies, waits for them, and re-layouts  9.71 us

profile of v1, /device:TPU:0, one launch (start us, length us, event | category | flops | bytes accessed | tf_op | source)
XLA Modules:
  0.0 45.6 jit_solution(3112711059872006994)
XLA Ops:
  0.6 1.3 %copy.13.dots = f32[1,7,128]{2,1,0:T(8,128)} copy(f32[1,7,128]{2,0,1:T(1,128)} %param.14) | data formatting | bytes 7168 | tf_op args[4]
  1.9 4.2 %copy.14.wq_in = bf16[2304,448]{1,0:T(8,128)(2,1)} copy(bf16[2304,448]{0,1:T(8,128)(2,1)} %param.18) | data formatting | bytes 4128768 | tf_op args[8]
  6.1 35.3 %shard_map.121 = (bf16[1,128,128]{2,1,0:T(8,128)(2,1)}, bf16[1,128,128]{2,1,0:T(8,128)(2,1)}, bf16[1,64,640]{2,1,0:T(8,128)(2,1)}) custom-call(bf16[1,128,896]{2,1,0:T(8,128)(2,1)} %q_in.1, bf16[1,128,128]{2,1,0:T(8,128)(2,1)} %k_in.1, bf16[1,128,128]{2,1,0:T(8,128)(2,1)} %v_in.1, bf16[1,128,896]{2,1,0:T(8,128)(2,1)} %g_in.1, f32[1,7,128]{2,1,0:T(8,128)} %copy.13.dots, ...), custom_call_target="tpu_custom_call" | custom-call | tf_op jit(solution)/shard_map/pallas_call | solution.py:284
  41.4 1.4 %copy.18 = bf16[1,128,128]{2,1,0:T(8,128)(2,1)} copy(bf16[1,128,128]{2,1,0:T(8,128)(2,1)} %get-tuple-element.6) | data formatting | bytes 65536
  42.7 1.4 %copy.19 = bf16[1,128,128]{2,1,0:T(8,128)(2,1)} copy(bf16[1,128,128]{2,1,0:T(8,128)(2,1)} %get-tuple-element.7) | data formatting | bytes 65536
  44.1 1.5 %copy.20 = bf16[1,64,640]{2,1,0:T(8,128)(2,1)} copy(bf16[1,64,640]{2,1,0:T(8,128)(2,1)} %get-tuple-element.8) | data formatting | bytes 163840

commit v2 on v1

--- a/solution.py
+++ b/solution.py
@@ -25,8 +25,8 @@
     n, sections, replicas,
     q_in, k_in, v_in, g_in, dots, frames, rows, source, wq_in, wp_in,
     dk_out, dv_out, patch_out,
-    qs, gs, kbuf, vbuf, sbuf, gsend, grecv, wq, wp, top, total, gq_acc, gqsel, kvsel, psend, precv,
-    load_sem, k_send, k_recv, v_send, v_recv, g_send, g_recv, a_send, a_recv, b_send, b_recv, p_send, p_recv,
+    qs, gs, qst, gst, kbuf, vbuf, sbuf, gsend, grecv, wq, wp, swapped, top, total, gq_acc, gqsel, kvsel, gradbuf, psend, precv,
+    load_sem, k_send, k_recv, v_send, v_recv, g_send, g_recv, a_send, a_recv, b_send, b_recv, p_send, p_recv, w_send, w_recv, s_send, s_recv,
 ):
     me = lax.axis_index("ctx")
     sec = lax.axis_index("section")
@@ -58,6 +58,13 @@
     def peer_back(a, b):
         return {"section": lax.rem(sec + a, sections), "dp": lax.rem(rep - b + replicas, replicas)}
 
+    core = lax.rem(rep, 2)
+    partner = {"dp": rep + 1 - 2 * core}
+    columns = wp.shape[1] // CHUNKS
+
+    def half_columns(which):
+        return pl.ds(pl.multiple_of(which * wp.shape[1], wp.shape[1]), wp.shape[1])
+
     barrier = pltpu.get_barrier_semaphore()
     each(1, n, lambda o: pl.semaphore_signal(barrier, inc=1, device_id=ahead(o), device_id_type=MESH))
     for a, b in plane:
@@ -67,7 +74,7 @@
         pltpu.make_async_copy(k_in.at[0], kbuf.at[0], load_sem.at[0]),
         pltpu.make_async_copy(v_in.at[0], vbuf.at[0], load_sem.at[1]),
         pltpu.make_async_copy(wq_in, wq, load_sem.at[2]),
-        pltpu.make_async_copy(wp_in, wp, load_sem.at[3]),
+        pltpu.make_async_copy(wp_in.at[:, half_columns(core)], wp, load_sem.at[3]),
     ]
     q_loads = [
         pltpu.make_async_copy(
@@ -105,15 +112,19 @@
     def g_copy(o):
         return remote(gsend.at[o], grecv.at[o], g_send.at[o], g_recv.at[o], behind(o))
 
+    mine_at = pl.ds(pl.multiple_of(rep * vis, vis), vis)
+
     def sel_copy(buf, send, recv, a, b):
-        return remote(
-            buf.at[0, pl.ds(0, vis)], buf.at[a, pl.ds(b * vis, vis)], send.at[a, b], recv.at[a, b], peer(a, b)
-        )
-
-    columns = wp.shape[1] // CHUNKS
+        return remote(buf.at[0, mine_at], buf.at[a, mine_at], send.at[a, b], recv.at[a, b], peer(a, b))
+
+    def weight_copy():
+        return remote(wp_in.at[:, half_columns(1 - core)], swapped, w_send.at[0], w_recv.at[0], partner)
+
+    def grad_copy():
+        return remote(gradbuf.at[0], gradbuf.at[1], s_send.at[0], s_recv.at[0], partner)
 
     def p_copy(i, a, b):
-        first = b * vis + lax.rem(sec + a, sections) * half
+        first = lax.rem(rep - b + replicas, replicas) * vis + lax.rem(sec + a, sections) * half
         return remote(
             psend.at[i, pl.ds(pl.multiple_of(first, half), half)],
             precv.at[i, a, b],
@@ -124,6 +135,7 @@
 
     each(1, n, lambda o: k_copy(o).start())
     each(1, n, lambda o: v_copy(o).start())
+    weight_copy().start()
 
     query_frames = frames[:, pl.ds(pl.multiple_of(me * tok, tok), tok)]
     row_at = lax.broadcasted_iota(jnp.int32, (tok, tok), 0)
@@ -131,7 +143,7 @@
     hot_t = (lax.broadcasted_iota(jnp.int32, (tok, vis), 0) == rows[0]).astype(F32).astype(BF)
     eye = (row_at == col_at).astype(F32).astype(BF)
     hot = dot(hot_t, eye, (0, 0)).astype(BF)
-    dots_row = jnp.concatenate([dots[0, h : h + 1, :] for h in range(GROUP)], axis=1)
+    dots_row = jnp.concatenate([dots[h] for h in range(GROUP)], axis=1)
 
     def bias_for(o):
         first = lax.rem(me - o + n, n) * tok
@@ -146,7 +158,7 @@
     gq_acc[...] = jnp.zeros_like(gq_acc)
 
     def first_pass(o):
-        s = dot(kbuf[o], qs[...], (1, 1)) + bias_for(o)
+        s = dot(kbuf[o], qst[...]) + bias_for(o)
         sbuf[o] = s
         top[...] = jnp.maximum(top[...], jnp.max(s, axis=0, keepdims=True))
 
@@ -155,9 +167,15 @@
         first_pass(o)
 
     loads[0].wait()
-    for c in q_loads:
+    for h, c in enumerate(q_loads):
         c.wait()
+        at = pl.ds(h * HEAD, HEAD)
+        qst[:, at] = jnp.transpose(qs[at, :])
     first_pass(0)
+    for h, c in enumerate(g_loads):
+        c.wait()
+        at = pl.ds(h * HEAD, HEAD)
+        gst[:, at] = jnp.transpose(gs[at, :])
     each(1, n, first_remote)
 
     def second_pass(o):
@@ -169,31 +187,30 @@
     total[...] = 1.0 / total[...]
 
     loads[1].wait()
-    for c in g_loads:
-        c.wait()
 
     def third_pass(o):
         p = sbuf[o] * total[...]
-        gp = dot(vbuf[o], gs[...], (1, 1))
+        gp = dot(vbuf[o], gst[...])
         gsc = (p * (gp - dots_row)).astype(BF)
         gv = dot(p.astype(BF), gs[...])
         gk = dot(gsc, qs[...]) * scale
         gq_acc[...] += dot(kbuf[o], gsc, (0, 0))
         return gk, gv
 
-    def third_remote(o):
+    def third_remote(at):
+        o = (at + n // 2 - 1) % (n - 1) + 1
         v_copy(o).wait_recv()
         gk, gv = third_pass(o)
         gsend[o, 0] = gk.astype(BF)
         gsend[o, 1] = gv.astype(BF)
         g_copy(o).start()
 
-    each(1, n, third_remote)
+    each(0, n - 1, third_remote)
     gk, gv = third_pass(0)
 
     gq = (gq_acc[...] * scale).astype(BF)
     for h in range(GROUP):
-        gqsel[0, 0:vis, h * HEAD : (h + 1) * HEAD] = dot(
+        gqsel[0, mine_at, h * HEAD : (h + 1) * HEAD] = dot(
             hot, gq[:, h * HEAD : (h + 1) * HEAD], (1, 1)
         ).astype(BF)
     for a, b in plane:
@@ -212,8 +229,8 @@
 
         gk, gv = lax.fori_loop(1, n, gather, (gk, gv))
     gk, gv = gk.astype(BF), gv.astype(BF)
-    kvsel[0, 0:vis, 0:HEAD] = dot(hot, gk).astype(BF)
-    kvsel[0, 0:vis, HEAD : 2 * HEAD] = dot(hot, gv).astype(BF)
+    kvsel[0, mine_at, 0:HEAD] = dot(hot, gk).astype(BF)
+    kvsel[0, mine_at, HEAD : 2 * HEAD] = dot(hot, gv).astype(BF)
     for a, b in plane:
         sel_copy(kvsel, b_send, b_recv, a, b).start()
     dk_out[0] = gk
@@ -227,47 +244,70 @@
 
     def weight_rows(a, offset, size):
         first = lax.rem(sec - a + sections, sections) * part + offset
-        return wq[pl.ds(pl.multiple_of(first, HEAD), size), :]
-
-    grad = dot(gqsel[0], weight_rows(0, 0, width))
+        return wq[:, pl.ds(pl.multiple_of(first, HEAD), size)]
+
+    grad = dot(weight_rows(0, 0, width), gqsel[0], (1, 1))
     for a in range(1, sections):
-        grad = grad + dot(gqsel[a], weight_rows(a, 0, width))
+        grad = grad + dot(weight_rows(a, 0, width), gqsel[a], (1, 1))
     for a, b in plane:
         sel_copy(kvsel, b_send, b_recv, a, b).wait_recv()
     for a in range(sections):
-        grad = grad + dot(kvsel[a], weight_rows(a, width, 2 * HEAD))
-    grad = grad.astype(BF)
-
+        grad = grad + dot(weight_rows(a, width, 2 * HEAD), kvsel[a], (1, 1))
+    gradbuf[0] = grad.astype(BF)
+    grad_copy().start()
+    own = dot(gradbuf[0], wp[...], (0, 0))
+    weight_copy().wait_recv()
+    grad_copy().wait_recv()
+    other = jnp.transpose(gradbuf[1])
     for i in range(CHUNKS):
-        psend[i] = dot(grad, wp[:, i * columns : (i + 1) * columns]).astype(BF)
+        at = slice(i * columns, (i + 1) * columns)
+        psend[i] = (own[:, at] + dot(other, swapped[:, at])).astype(BF)
         for a, b in plane:
             p_copy(i, a, b).start()
 
     slots = source.shape[2]
-    quarter = wp.shape[1] // 4
     at = lax.broadcasted_iota(jnp.int32, (slots, slots), 0)
     slot_of = lax.rem(at, half) * 4 + lax.div(at, half)
     moved_t = (slot_of == source[0]).astype(F32).astype(BF)
 
-    pieces = []
+    near, far = [], []
     for i in range(CHUNKS):
-        mine = psend[i, pl.ds(pl.multiple_of(sec * half, half), half), :].astype(F32)
+        even = psend[i, pl.ds(pl.multiple_of(rep * vis + sec * half, half), half), :].astype(F32)
+        odd = jnp.zeros_like(even)
         for a, b in plane:
             p_copy(i, a, b).wait_recv()
-            mine = mine + precv[i, a, b].astype(F32)
-        for c in range(columns // quarter):
-            pieces.append(mine[:, c * quarter : (c + 1) * quarter])
+            if b % 2:
+                odd = odd + precv[i, a, b].astype(F32)
+            else:
+                even = even + precv[i, a, b].astype(F32)
+        near.append(even)
+        far.append(odd)
+    first = [jnp.where(core == 0, x, y) for x, y in zip(near, far)]
+    second = [jnp.where(core == 0, y, x) for x, y in zip(near, far)]
+    pieces = first + second
     merged = jnp.concatenate(pieces, axis=0).astype(BF)
     patch_out[0] = dot(moved_t, merged, (0, 0)).astype(BF)
 
     each(1, n, lambda o: k_copy(o).wait_send())
     each(1, n, lambda o: v_copy(o).wait_send())
     each(1, n, lambda o: g_copy(o).wait_send())
+    weight_copy().wait_send()
+    grad_copy().wait_send()
     for a, b in plane:
         sel_copy(gqsel, a_send, a_recv, a, b).wait_send()
         sel_copy(kvsel, b_send, b_recv, a, b).wait_send()
         for i in range(CHUNKS):
             p_copy(i, a, b).wait_send()
+
+
+def hand_on(a, b, c, a_out, b_out, c_out, sems):
+    copies = [
+        pltpu.make_async_copy(x, y, sems.at[i]) for i, (x, y) in enumerate(((a, a_out), (b, b_out), (c, c_out)))
+    ]
+    for copy in copies:
+        copy.start()
+    for copy in copies:
+        copy.wait()
 
 
 def solution(mesh):
@@ -281,42 +321,56 @@
         anywhere = pl.BlockSpec(memory_space=pl.ANY)
         inside = pl.BlockSpec(memory_space=pltpu.VMEM)
         dma = pltpu.SemaphoreType.DMA
-        return pl.pallas_call(
+        model, side = wp.shape[0], wp.shape[1] // 2
+        shapes = (
+            jax.ShapeDtypeStruct(k.shape, BF),
+            jax.ShapeDtypeStruct(v.shape, BF),
+            jax.ShapeDtypeStruct((1, slots, quarter), BF),
+        )
+        outs = pl.pallas_call(
             functools.partial(kernel, n, sections, replicas),
-            out_shape=(
-                jax.ShapeDtypeStruct(k.shape, BF),
-                jax.ShapeDtypeStruct(v.shape, BF),
-                jax.ShapeDtypeStruct((1, slots, quarter), BF),
-            ),
+            out_shape=shapes,
             in_specs=[anywhere] * 4 + [inside] * 4 + [anywhere] * 2,
             out_specs=(inside, inside, inside),
             scratch_shapes=[
                 pltpu.VMEM((width, HEAD), BF),
                 pltpu.VMEM((width, HEAD), BF),
+                pltpu.VMEM((HEAD, width), BF),
+                pltpu.VMEM((HEAD, width), BF),
                 pltpu.VMEM((n, tok, HEAD), BF),
                 pltpu.VMEM((n, tok, HEAD), BF),
                 pltpu.VMEM((n, tok, width), F32),
                 pltpu.VMEM((n, 2, tok, HEAD), BF),
                 pltpu.VMEM((n, 2, tok, HEAD), BF),
-                pltpu.VMEM(wq.shape, BF),
-                pltpu.VMEM(wp.shape, BF),
+                pltpu.VMEM((model, wq.shape[0]), BF),
+                pltpu.VMEM((model, side), BF),
+                pltpu.VMEM((model, side), BF),
                 pltpu.VMEM((1, width), F32),
                 pltpu.VMEM((1, width), F32),
                 pltpu.VMEM((HEAD, width), F32),
                 pltpu.VMEM((sections, replicas * vis, width), BF),
                 pltpu.VMEM((sections, replicas * vis, 2 * HEAD), BF),
-                pltpu.VMEM((CHUNKS, replicas * vis, wp.shape[1] // CHUNKS), BF),
-                pltpu.VMEM((CHUNKS, sections, replicas, half, wp.shape[1] // CHUNKS), BF),
+                pltpu.VMEM((2, model, replicas * vis), BF),
+                pltpu.VMEM((CHUNKS, replicas * vis, side // CHUNKS), BF),
+                pltpu.VMEM((CHUNKS, sections, replicas, half, side // CHUNKS), BF),
                 dma((4 + 2 * GROUP,)),
                 dma((n,)), dma((n,)), dma((n,)), dma((n,)), dma((n,)), dma((n,)),
                 dma((sections, replicas)), dma((sections, replicas)),
                 dma((sections, replicas)), dma((sections, replicas)),
                 dma((CHUNKS, sections, replicas)), dma((CHUNKS, sections, replicas)),
+                dma((1,)), dma((1,)), dma((1,)), dma((1,)),
             ],
             compiler_params=pltpu.CompilerParams(
                 collective_id=0, has_side_effects=True, vmem_limit_bytes=56 * 1024 * 1024
             ),
-        )(q, k, v, g, dots, frames, rows, source, wq, wp)
+        )(q, k, v, g, dots.transpose(1, 0, 2), frames, rows, source, wq.T, wp)
+        return pl.pallas_call(
+            hand_on,
+            out_shape=shapes,
+            in_specs=[pl.BlockSpec(memory_space=pltpu.HBM)] * 3,
+            out_specs=(pl.BlockSpec(memory_space=pltpu.HBM),) * 3,
+            scratch_shapes=[dma((3,))],
+        )(*outs)
 
     placed = (
         P("dp", "ctx", "section"),

time: 46 us -> 39.2 us (0.85)
  local copies, waits for them, and re-layouts: 9.71 us -> 0 us
  Pallas kernels: 35.3 us -> 38.4 us
    unnamed x5 -> x0, local copies, waits for them, and re-layouts: 9.71 us -> none
    pallas_call x0 -> x1, Pallas kernels: none -> 5.6 us  [shards(): pl.pallas_call(hand_on, out_shape=shapes, in_specs=[pl.BlockSpec(memory_s...]
    pallas_call x1, Pallas kernels: 35.3 us -> 32.8 us  [shards(): pl.pallas_call(functools.partial(kernel, n, sections, replicas), out_shap...]
where the time goes in v2:
time: 39.2 us; the launch traced here: 39 us
  Pallas kernels  38.4 us (98%)
  between operations  0.64 us (2%)
    pallas_call x1, Pallas kernels, shards(): pl.pallas_call(functools.partial(kernel, n, sections, replicas), out_shap...  32.8 us
    pallas_call x1, Pallas kernels, shards(): pl.pallas_call(hand_on, out_shape=shapes, in_specs=[pl.BlockSpec(memory_s...  5.6 us

profile of v2, /device:TPU:0, one launch (start us, length us, event | category | flops | bytes accessed | tf_op | source)
XLA Modules:
  0.0 39.0 jit_solution(17970373191385885996)
XLA Ops:
  0.6 32.8 %shard_map.121 = (bf16[1,128,128]{2,1,0:T(8,128)(2,1)}, bf16[1,128,128]{2,1,0:T(8,128)(2,1)}, bf16[1,64,640]{2,1,0:T(8,128)(2,1)}) custom-call(bf16[1,128,896]{2,1,0:T(8,128)(2,1)} %q_in.1, bf16[1,128,128]{2,1,0:T(8,128)(2,1)} %k_in.1, bf16[1,128,128]{2,1,0:T(8,128)(2,1)} %v_in.1, bf16[1,128,896]{2,1,0:T(8,128)(2,1)} %g_in.1, f32[7,1,128]{2,1,0:T(1,128)} %bitcast.3, ...), custom_call_target="tpu_custom_call" | custom-call | tf_op jit(solution)/shard_map/pallas_call | solution.py:330
  33.4 5.6 %shard_map.122 = (bf16[1,128,128]{2,1,0:T(8,128)(2,1)}, bf16[1,128,128]{2,1,0:T(8,128)(2,1)}, bf16[1,64,640]{2,1,0:T(8,128)(2,1)}) custom-call(bf16[1,128,128]{2,1,0:T(8,128)(2,1)} %get-tuple-element.6.a, bf16[1,128,128]{2,1,0:T(8,128)(2,1)} %get-tuple-element.7.b, bf16[1,64,640]{2,1,0:T(8,128)(2,1)} %get-tuple-element.8.c), custom_call_target="tpu_custom_call" | custom-call | tf_op jit(solution)/shard_map/pallas_call | solution.py:367

commit v3 on v2

--- a/solution.py
+++ b/solution.py
@@ -25,8 +25,8 @@
     n, sections, replicas,
     q_in, k_in, v_in, g_in, dots, frames, rows, source, wq_in, wp_in,
     dk_out, dv_out, patch_out,
-    qs, gs, qst, gst, kbuf, vbuf, sbuf, gsend, grecv, wq, wp, swapped, top, total, gq_acc, gqsel, kvsel, gradbuf, psend, precv,
-    load_sem, k_send, k_recv, v_send, v_recv, g_send, g_recv, a_send, a_recv, b_send, b_recv, p_send, p_recv, w_send, w_recv, s_send, s_recv,
+    qs, gs, qst, gst, kbuf, vbuf, sbuf, gsend, grecv, hots, rsend, rrecv, wq, wp, swapped, top, total, gq_acc, gqsel, kvsel, gradbuf, psend, precv,
+    load_sem, k_send, k_recv, v_send, v_recv, g_send, g_recv, a_send, a_recv, b_send, b_recv, p_send, p_recv, w_send, w_recv, s_send, s_recv, h_send, h_recv, r_send, r_recv,
 ):
     me = lax.axis_index("ctx")
     sec = lax.axis_index("section")
@@ -112,6 +112,17 @@
     def g_copy(o):
         return remote(gsend.at[o], grecv.at[o], g_send.at[o], g_recv.at[o], behind(o))
 
+    def h_copy(o):
+        return remote(hots.at[0], hots.at[o], h_send.at[o], h_recv.at[o], ahead(o))
+
+    def r_copy(o):
+        return remote(rsend.at[o], rrecv.at[o], r_send.at[o], r_recv.at[o], behind(o))
+
+    def pass_copy(a, b):
+        at = pl.ds(pl.multiple_of(lax.rem(rep - b + replicas, replicas) * vis, vis), vis)
+        return remote(gqsel.at[a, at], gqsel.at[a, at], a_send.at[a, b + 1], a_recv.at[a, b + 1], partner)
+
+    across = [(a, b) for a, b in plane if b % 2 == 0]
     mine_at = pl.ds(pl.multiple_of(rep * vis, vis), vis)
 
     def sel_copy(buf, send, recv, a, b):
@@ -143,6 +154,8 @@
     hot_t = (lax.broadcasted_iota(jnp.int32, (tok, vis), 0) == rows[0]).astype(F32).astype(BF)
     eye = (row_at == col_at).astype(F32).astype(BF)
     hot = dot(hot_t, eye, (0, 0)).astype(BF)
+    hots[0] = hot
+    each(1, n, lambda o: h_copy(o).start())
     dots_row = jnp.concatenate([dots[h] for h in range(GROUP)], axis=1)
 
     def bias_for(o):
@@ -200,10 +213,14 @@
     def third_remote(at):
         o = (at + n // 2 - 1) % (n - 1) + 1
         v_copy(o).wait_recv()
+        h_copy(o).wait_recv()
         gk, gv = third_pass(o)
-        gsend[o, 0] = gk.astype(BF)
-        gsend[o, 1] = gv.astype(BF)
-        g_copy(o).start()
+        gk, gv = gk.astype(BF), gv.astype(BF)
+        gsend[o, 0] = gk
+        gsend[o, 1] = gv
+        rsend[o, :, 0:HEAD] = dot(hots[o], gk).astype(BF)
+        rsend[o, :, HEAD : 2 * HEAD] = dot(hots[o], gv).astype(BF)
+        r_copy(o).start()
 
     each(0, n - 1, third_remote)
     gk, gv = third_pass(0)
@@ -213,34 +230,45 @@
         gqsel[0, mine_at, h * HEAD : (h + 1) * HEAD] = dot(
             hot, gq[:, h * HEAD : (h + 1) * HEAD], (1, 1)
         ).astype(BF)
-    for a, b in plane:
+    for a, b in across:
         sel_copy(gqsel, a_send, a_recv, a, b).start()
-
-    if n <= 8:
-        for o in range(1, n):
-            g_copy(o).wait_recv()
-            gk = gk + grecv[o, 0].astype(F32)
-            gv = gv + grecv[o, 1].astype(F32)
-    else:
-
-        def gather(o, pair):
-            g_copy(o).wait_recv()
-            return pair[0] + grecv[o, 0].astype(F32), pair[1] + grecv[o, 1].astype(F32)
-
-        gk, gv = lax.fori_loop(1, n, gather, (gk, gv))
-    gk, gv = gk.astype(BF), gv.astype(BF)
-    kvsel[0, mine_at, 0:HEAD] = dot(hot, gk).astype(BF)
-    kvsel[0, mine_at, HEAD : 2 * HEAD] = dot(hot, gv).astype(BF)
+    pass_copy(0, 0).start()
+    each(1, n, lambda o: g_copy(o).start())
+
+    def picked(x):
+        return lax.dot_general(
+            hot.astype(F32), x, (((1,), (0,)), ((), ())),
+            precision=lax.Precision.HIGHEST, preferred_element_type=F32,
+        )
+
+    def gather(copy, read, start):
+        def step(o, pair):
+            copy(o).wait_recv()
+            x, y = read(o)
+            return pair[0] + x.astype(F32), pair[1] + y.astype(F32)
+
+        if n <= 8:
+            for o in range(1, n):
+                start = step(o, start)
+            return start
+        return lax.fori_loop(1, n, step, start)
+
+    rows_k, rows_v = gather(
+        r_copy, lambda o: (rrecv[o, :, 0:HEAD], rrecv[o, :, HEAD : 2 * HEAD]), (picked(gk), picked(gv))
+    )
+    kvsel[0, mine_at, 0:HEAD] = rows_k.astype(BF)
+    kvsel[0, mine_at, HEAD : 2 * HEAD] = rows_v.astype(BF)
     for a, b in plane:
         sel_copy(kvsel, b_send, b_recv, a, b).start()
-    dk_out[0] = gk
-    dv_out[0] = gv
+    for a, b in across:
+        sel_copy(gqsel, a_send, a_recv, a, b).wait_recv()
+        pass_copy(a, b).start()
 
     loads[2].wait()
     loads[3].wait()
     part = width + 2 * HEAD
-    for a, b in plane:
-        sel_copy(gqsel, a_send, a_recv, a, b).wait_recv()
+    for a, b in [(0, 0)] + across:
+        pass_copy(a, b).wait_recv()
 
     def weight_rows(a, offset, size):
         first = lax.rem(sec - a + sections, sections) * part + offset
@@ -265,6 +293,10 @@
         for a, b in plane:
             p_copy(i, a, b).start()
 
+    gk, gv = gather(g_copy, lambda o: (grecv[o, 0], grecv[o, 1]), (gk, gv))
+    dk_out[0] = gk.astype(BF)
+    dv_out[0] = gv.astype(BF)
+
     slots = source.shape[2]
     at = lax.broadcasted_iota(jnp.int32, (slots, slots), 0)
     slot_of = lax.rem(at, half) * 4 + lax.div(at, half)
@@ -291,23 +323,24 @@
     each(1, n, lambda o: k_copy(o).wait_send())
     each(1, n, lambda o: v_copy(o).wait_send())
     each(1, n, lambda o: g_copy(o).wait_send())
+    each(1, n, lambda o: h_copy(o).wait_send())
+    each(1, n, lambda o: r_copy(o).wait_send())
+    pass_copy(0, 0).wait_send()
+    for a, b in across:
+        sel_copy(gqsel, a_send, a_recv, a, b).wait_send()
+        pass_copy(a, b).wait_send()
     weight_copy().wait_send()
     grad_copy().wait_send()
     for a, b in plane:
-        sel_copy(gqsel, a_send, a_recv, a, b).wait_send()
         sel_copy(kvsel, b_send, b_recv, a, b).wait_send()
         for i in range(CHUNKS):
             p_copy(i, a, b).wait_send()
 
 
-def hand_on(a, b, c, a_out, b_out, c_out, sems):
-    copies = [
-        pltpu.make_async_copy(x, y, sems.at[i]) for i, (x, y) in enumerate(((a, a_out), (b, b_out), (c, c_out)))
-    ]
-    for copy in copies:
-        copy.start()
-    for copy in copies:
-        copy.wait()
+def hand_on(a, b, c, a_out, b_out, c_out):
+    a_out[...] = a[...]
+    b_out[...] = b[...]
+    c_out[...] = c[...]
 
 
 def solution(mesh):
@@ -342,6 +375,9 @@
                 pltpu.VMEM((n, tok, width), F32),
                 pltpu.VMEM((n, 2, tok, HEAD), BF),
                 pltpu.VMEM((n, 2, tok, HEAD), BF),
+                pltpu.VMEM((n, vis, tok), BF),
+                pltpu.VMEM((n, vis, 2 * HEAD), BF),
+                pltpu.VMEM((n, vis, 2 * HEAD), BF),
                 pltpu.VMEM((model, wq.shape[0]), BF),
                 pltpu.VMEM((model, side), BF),
                 pltpu.VMEM((model, side), BF),
@@ -359,6 +395,7 @@
                 dma((sections, replicas)), dma((sections, replicas)),
                 dma((CHUNKS, sections, replicas)), dma((CHUNKS, sections, replicas)),
                 dma((1,)), dma((1,)), dma((1,)), dma((1,)),
+                dma((n,)), dma((n,)), dma((n,)), dma((n,)),
             ],
             compiler_params=pltpu.CompilerParams(
                 collective_id=0, has_side_effects=True, vmem_limit_bytes=56 * 1024 * 1024
@@ -367,9 +404,8 @@
         return pl.pallas_call(
             hand_on,
             out_shape=shapes,
-            in_specs=[pl.BlockSpec(memory_space=pltpu.HBM)] * 3,
-            out_specs=(pl.BlockSpec(memory_space=pltpu.HBM),) * 3,
-            scratch_shapes=[dma((3,))],
+            in_specs=[inside] * 3,
+            out_specs=(inside,) * 3,
         )(*outs)
 
     placed = (

time: 39.2 us -> 34.8 us (0.89)
  Pallas kernels: 38.4 us -> 34 us
    pallas_call x1, Pallas kernels: 5.6 us -> 1.59 us  [shards(): pl.pallas_call(hand_on, out_shape=shapes, in_specs=[inside] * 3, out_spec...]
where the time goes in v3:
time: 34.8 us; the launch traced here: 34.6 us
  Pallas kernels  34 us (98%)
  between operations  0.64 us (2%)
    pallas_call x1, Pallas kernels, shards(): pl.pallas_call(functools.partial(kernel, n, sections, replicas), out_shap...  32.4 us
    pallas_call x1, Pallas kernels, shards(): pl.pallas_call(hand_on, out_shape=shapes, in_specs=[inside] * 3, out_spec...  1.59 us

profile of v3, /device:TPU:0, one launch (start us, length us, event | category | flops | bytes accessed | tf_op | source)
XLA Modules:
  0.0 34.6 jit_solution(16681582898653999149)
XLA Ops:
  0.6 32.4 %shard_map.121 = (bf16[1,128,128]{2,1,0:T(8,128)(2,1)}, bf16[1,128,128]{2,1,0:T(8,128)(2,1)}, bf16[1,64,640]{2,1,0:T(8,128)(2,1)}) custom-call(bf16[1,128,896]{2,1,0:T(8,128)(2,1)} %q_in.1, bf16[1,128,128]{2,1,0:T(8,128)(2,1)} %k_in.1, bf16[1,128,128]{2,1,0:T(8,128)(2,1)} %v_in.1, bf16[1,128,896]{2,1,0:T(8,128)(2,1)} %g_in.1, f32[7,1,128]{2,1,0:T(1,128)} %bitcast.3, ...), custom_call_target="tpu_custom_call" | custom-call | tf_op jit(solution)/shard_map/pallas_call | solution.py:363
  33.0 1.6 %shard_map.122 = (bf16[1,128,128]{2,1,0:T(8,128)(2,1)}, bf16[1,128,128]{2,1,0:T(8,128)(2,1)}, bf16[1,64,640]{2,1,0:T(8,128)(2,1)}) custom-call(bf16[1,128,128]{2,1,0:T(8,128)(2,1)} %get-tuple-element.6.a, bf16[1,128,128]{2,1,0:T(8,128)(2,1)} %get-tuple-element.7.b, bf16[1,64,640]{2,1,0:T(8,128)(2,1)} %get-tuple-element.8.c), custom_call_target="tpu_custom_call" | custom-call | tf_op jit(solution)/shard_map/pallas_call | solution.py:404

commit v4 on v3

--- a/solution.py
+++ b/solution.py
@@ -23,9 +23,9 @@
 
 def kernel(
     n, sections, replicas,
-    q_in, k_in, v_in, g_in, dots, frames, rows, source, wq_in, wp_in,
+    q_in, k_in, v_in, g_in, dots_in, frames_in, rows_in, source_in, wq_in, wp_in,
     dk_out, dv_out, patch_out,
-    qs, gs, qst, gst, kbuf, vbuf, sbuf, gsend, grecv, hots, rsend, rrecv, wq, wp, swapped, top, total, gq_acc, gqsel, kvsel, gradbuf, psend, precv,
+    dots, frames, rows, source, qs, gs, qst, gst, kbuf, vbuf, sbuf, gsend, grecv, hots, rsend, rrecv, wq, wp, swapped, top, total, gq_acc, gqsel, kvsel, gradbuf, psend, precv,
     load_sem, k_send, k_recv, v_send, v_recv, g_send, g_recv, a_send, a_recv, b_send, b_recv, p_send, p_recv, w_send, w_recv, s_send, s_recv, h_send, h_recv, r_send, r_recv,
 ):
     me = lax.axis_index("ctx")
@@ -33,6 +33,7 @@
     rep = lax.axis_index("dp")
     tok = k_in.shape[1]
     vis = rows.shape[2]
+    unrolled = n <= 8
     half = vis // 2
     width = GROUP * HEAD
     scale = 1.0 / math.sqrt(HEAD)
@@ -88,7 +89,13 @@
         )
         for h in range(GROUP)
     ]
+    small = [
+        pltpu.make_async_copy(x, y, load_sem.at[4 + 2 * GROUP + i])
+        for i, (x, y) in enumerate(((frames_in, frames), (rows_in, rows), (dots_in, dots), (source_in, source)))
+    ]
     loads[0].start()
+    for c in small:
+        c.start()
     for c in q_loads:
         c.start()
     loads[1].start()
@@ -148,6 +155,8 @@
     each(1, n, lambda o: v_copy(o).start())
     weight_copy().start()
 
+    for c in small:
+        c.wait()
     query_frames = frames[:, pl.ds(pl.multiple_of(me * tok, tok), tok)]
     row_at = lax.broadcasted_iota(jnp.int32, (tok, tok), 0)
     col_at = lax.broadcasted_iota(jnp.int32, (tok, tok), 1)
@@ -163,33 +172,43 @@
         line = frames[:, pl.ds(pl.multiple_of(first, tok), tok)].astype(F32)
         key_frames = jnp.transpose(jnp.broadcast_to(line, (tok, tok)))
         allowed = (first + row_at <= me * tok + col_at) | (key_frames == query_frames.astype(F32))
-        bias = jnp.where(allowed, 0.0, MASKED)
+        return jnp.where(allowed, 0.0, MASKED)
+
+    def wide(bias):
         return jnp.concatenate([bias] * GROUP, axis=1)
 
     top[...] = jnp.full_like(top, MASKED)
     total[...] = jnp.zeros_like(total)
     gq_acc[...] = jnp.zeros_like(gq_acc)
 
-    def first_pass(o):
-        s = dot(kbuf[o], qst[...]) + bias_for(o)
+    def first_pass(o, s, bias):
+        s = s + wide(bias)
         sbuf[o] = s
         top[...] = jnp.maximum(top[...], jnp.max(s, axis=0, keepdims=True))
 
     def first_remote(o):
         k_copy(o).wait_recv()
-        first_pass(o)
-
+        first_pass(o, dot(kbuf[o], qst[...]), bias_for(o))
+
+    biases = [bias_for(o) for o in range(n if unrolled else 1)]
     loads[0].wait()
     for h, c in enumerate(q_loads):
         c.wait()
         at = pl.ds(h * HEAD, HEAD)
         qst[:, at] = jnp.transpose(qs[at, :])
-    first_pass(0)
+    first_pass(0, dot(kbuf[0], qst[...]), biases[0])
     for h, c in enumerate(g_loads):
         c.wait()
         at = pl.ds(h * HEAD, HEAD)
         gst[:, at] = jnp.transpose(gs[at, :])
-    each(1, n, first_remote)
+    if unrolled:
+        for o in range(1, n):
+            k_copy(o).wait_recv()
+        s = dot(kbuf[1:n].reshape((n - 1) * tok, HEAD), qst[...])
+        for o in range(1, n):
+            first_pass(o, s[(o - 1) * tok : o * tok], biases[o])
+    else:
+        lax.fori_loop(1, n, lambda o, c: (first_remote(o), c)[1], 0)
 
     def second_pass(o):
         e = jnp.exp2((sbuf[o] - top[...]) * factor)
@@ -201,29 +220,39 @@
 
     loads[1].wait()
 
-    def third_pass(o):
-        p = sbuf[o] * total[...]
-        gp = dot(vbuf[o], gst[...])
+    def third_pass(p, values):
+        gp = dot(values, gst[...])
         gsc = (p * (gp - dots_row)).astype(BF)
-        gv = dot(p.astype(BF), gs[...])
-        gk = dot(gsc, qs[...]) * scale
-        gq_acc[...] += dot(kbuf[o], gsc, (0, 0))
-        return gk, gv
-
-    def third_remote(at):
-        o = (at + n // 2 - 1) % (n - 1) + 1
-        v_copy(o).wait_recv()
-        h_copy(o).wait_recv()
-        gk, gv = third_pass(o)
+        return gsc, dot(gsc, qs[...]) * scale, dot(p.astype(BF), gs[...])
+
+    def send_rows(o, gk, gv):
         gk, gv = gk.astype(BF), gv.astype(BF)
         gsend[o, 0] = gk
         gsend[o, 1] = gv
-        rsend[o, :, 0:HEAD] = dot(hots[o], gk).astype(BF)
-        rsend[o, :, HEAD : 2 * HEAD] = dot(hots[o], gv).astype(BF)
+        rsend[o] = dot(hots[o], jnp.concatenate([gk, gv], axis=1)).astype(BF)
         r_copy(o).start()
 
-    each(0, n - 1, third_remote)
-    gk, gv = third_pass(0)
+    def third_remote(o):
+        v_copy(o).wait_recv()
+        h_copy(o).wait_recv()
+        gsc, gk, gv = third_pass(sbuf[o] * total[...], vbuf[o])
+        gq_acc[...] += dot(kbuf[o], gsc, (0, 0))
+        send_rows(o, gk, gv)
+
+    if unrolled:
+        for o in range(1, n):
+            v_copy(o).wait_recv()
+            h_copy(o).wait_recv()
+        keys, values = kbuf[...].reshape(n * tok, HEAD), vbuf[...].reshape(n * tok, HEAD)
+        gsc, gk_all, gv_all = third_pass(sbuf[...].reshape(n * tok, width) * total[...], values)
+        for o in range(1, n):
+            send_rows(o, gk_all[o * tok : (o + 1) * tok], gv_all[o * tok : (o + 1) * tok])
+        gk, gv = gk_all[0:tok], gv_all[0:tok]
+        gq_acc[...] = dot(keys, gsc, (0, 0))
+    else:
+        lax.fori_loop(1, n, lambda o, c: (third_remote(o), c)[1], 0)
+        gsc, gk, gv = third_pass(sbuf[0] * total[...], vbuf[0])
+        gq_acc[...] += dot(kbuf[0], gsc, (0, 0))
 
     gq = (gq_acc[...] * scale).astype(BF)
     for h in range(GROUP):
@@ -363,9 +392,13 @@
         outs = pl.pallas_call(
             functools.partial(kernel, n, sections, replicas),
             out_shape=shapes,
-            in_specs=[anywhere] * 4 + [inside] * 4 + [anywhere] * 2,
+            in_specs=[anywhere] * 10,
             out_specs=(inside, inside, inside),
             scratch_shapes=[
+                pltpu.VMEM((GROUP, 1, tok), F32),
+                pltpu.VMEM(frames.shape, jnp.int32),
+                pltpu.VMEM(rows.shape, jnp.int32),
+                pltpu.VMEM(source.shape, jnp.int32),
                 pltpu.VMEM((width, HEAD), BF),
                 pltpu.VMEM((width, HEAD), BF),
                 pltpu.VMEM((HEAD, width), BF),
@@ -389,7 +422,7 @@
                 pltpu.VMEM((2, model, replicas * vis), BF),
                 pltpu.VMEM((CHUNKS, replicas * vis, side // CHUNKS), BF),
                 pltpu.VMEM((CHUNKS, sections, replicas, half, side // CHUNKS), BF),
-                dma((4 + 2 * GROUP,)),
+                dma((8 + 2 * GROUP,)),
                 dma((n,)), dma((n,)), dma((n,)), dma((n,)), dma((n,)), dma((n,)),
                 dma((sections, replicas)), dma((sections, replicas)),
                 dma((sections, replicas)), dma((sections, replicas)),

time: 34.8 us -> 34.7 us (level)
  no operation moved by 1% of the time
where the time goes in v4:
time: 34.7 us; the launch traced here: 34.5 us
  Pallas kernels  33.9 us (98%)
  between operations  0.64 us (2%)
    pallas_call x1, Pallas kernels, shards(): pl.pallas_call(functools.partial(kernel, n, sections, replicas), out_shap...  32.3 us
    pallas_call x1, Pallas kernels, shards(): pl.pallas_call(hand_on, out_shape=shapes, in_specs=[inside] * 3, out_spec...  1.59 us

profile of v4, /device:TPU:0, one launch (start us, length us, event | category | flops | bytes accessed | tf_op | source)
XLA Modules:
  0.0 34.5 jit_solution(13729943974076760084)
XLA Ops:
  0.6 32.3 %shard_map.121 = (bf16[1,128,128]{2,1,0:T(8,128)(2,1)}, bf16[1,128,128]{2,1,0:T(8,128)(2,1)}, bf16[1,64,640]{2,1,0:T(8,128)(2,1)}) custom-call(bf16[1,128,896]{2,1,0:T(8,128)(2,1)} %q_in.1, bf16[1,128,128]{2,1,0:T(8,128)(2,1)} %k_in.1, bf16[1,128,128]{2,1,0:T(8,128)(2,1)} %v_in.1, bf16[1,128,896]{2,1,0:T(8,128)(2,1)} %g_in.1, f32[7,1,128]{2,1,0:T(1,128)} %bitcast.3, ...), custom_call_target="tpu_custom_call" | custom-call | tf_op jit(solution)/shard_map/pallas_call | solution.py:392
  32.9 1.6 %shard_map.122 = (bf16[1,128,128]{2,1,0:T(8,128)(2,1)}, bf16[1,128,128]{2,1,0:T(8,128)(2,1)}, bf16[1,64,640]{2,1,0:T(8,128)(2,1)}) custom-call(bf16[1,128,128]{2,1,0:T(8,128)(2,1)} %get-tuple-element.6.a, bf16[1,128,128]{2,1,0:T(8,128)(2,1)} %get-tuple-element.7.b, bf16[1,64,640]{2,1,0:T(8,128)(2,1)} %get-tuple-element.8.c), custom_call_target="tpu_custom_call" | custom-call | tf_op jit(solution)/shard_map/pallas_call | solution.py:437

commit v5 on v4

--- a/solution.py
+++ b/solution.py
@@ -12,7 +12,7 @@
 GROUP = 7
 MASKED = -1e30
 MESH = pl.DeviceIdType.MESH
-CHUNKS = 2
+CHUNKS = 4
 BF = jnp.bfloat16
 F32 = jnp.float32
 
@@ -25,8 +25,8 @@
     n, sections, replicas,
     q_in, k_in, v_in, g_in, dots_in, frames_in, rows_in, source_in, wq_in, wp_in,
     dk_out, dv_out, patch_out,
-    dots, frames, rows, source, qs, gs, qst, gst, kbuf, vbuf, sbuf, gsend, grecv, hots, rsend, rrecv, wq, wp, swapped, top, total, gq_acc, gqsel, kvsel, gradbuf, psend, precv,
-    load_sem, k_send, k_recv, v_send, v_recv, g_send, g_recv, a_send, a_recv, b_send, b_recv, p_send, p_recv, w_send, w_recv, s_send, s_recv, h_send, h_recv, r_send, r_recv,
+    dots, frames, rows, source, qs, gs, qst, gst, kbuf, vbuf, sbuf, gsend, grecv, hots, rsend, rrecv, wq, wp, top, total, gq_acc, gqsel, kvsel, psend, precv,
+    load_sem, k_send, k_recv, v_send, v_recv, g_send, g_recv, a_send, a_recv, b_send, b_recv, p_send, p_recv, h_send, h_recv, r_send, r_recv,
 ):
     me = lax.axis_index("ctx")
     sec = lax.axis_index("section")
@@ -63,9 +63,6 @@
     partner = {"dp": rep + 1 - 2 * core}
     columns = wp.shape[1] // CHUNKS
 
-    def half_columns(which):
-        return pl.ds(pl.multiple_of(which * wp.shape[1], wp.shape[1]), wp.shape[1])
-
     barrier = pltpu.get_barrier_semaphore()
     each(1, n, lambda o: pl.semaphore_signal(barrier, inc=1, device_id=ahead(o), device_id_type=MESH))
     for a, b in plane:
@@ -75,7 +72,7 @@
         pltpu.make_async_copy(k_in.at[0], kbuf.at[0], load_sem.at[0]),
         pltpu.make_async_copy(v_in.at[0], vbuf.at[0], load_sem.at[1]),
         pltpu.make_async_copy(wq_in, wq, load_sem.at[2]),
-        pltpu.make_async_copy(wp_in.at[:, half_columns(core)], wp, load_sem.at[3]),
+        pltpu.make_async_copy(wp_in, wp, load_sem.at[3]),
     ]
     q_loads = [
         pltpu.make_async_copy(
@@ -135,12 +132,6 @@
     def sel_copy(buf, send, recv, a, b):
         return remote(buf.at[0, mine_at], buf.at[a, mine_at], send.at[a, b], recv.at[a, b], peer(a, b))
 
-    def weight_copy():
-        return remote(wp_in.at[:, half_columns(1 - core)], swapped, w_send.at[0], w_recv.at[0], partner)
-
-    def grad_copy():
-        return remote(gradbuf.at[0], gradbuf.at[1], s_send.at[0], s_recv.at[0], partner)
-
     def p_copy(i, a, b):
         first = lax.rem(rep - b + replicas, replicas) * vis + lax.rem(sec + a, sections) * half
         return remote(
@@ -153,7 +144,6 @@
 
     each(1, n, lambda o: k_copy(o).start())
     each(1, n, lambda o: v_copy(o).start())
-    weight_copy().start()
 
     for c in small:
         c.wait()
@@ -310,15 +300,10 @@
         sel_copy(kvsel, b_send, b_recv, a, b).wait_recv()
     for a in range(sections):
         grad = grad + dot(weight_rows(a, width, 2 * HEAD), kvsel[a], (1, 1))
-    gradbuf[0] = grad.astype(BF)
-    grad_copy().start()
-    own = dot(gradbuf[0], wp[...], (0, 0))
-    weight_copy().wait_recv()
-    grad_copy().wait_recv()
-    other = jnp.transpose(gradbuf[1])
+    grad = jnp.transpose(grad.astype(BF))
     for i in range(CHUNKS):
         at = slice(i * columns, (i + 1) * columns)
-        psend[i] = (own[:, at] + dot(other, swapped[:, at])).astype(BF)
+        psend[i] = dot(grad, wp[:, at]).astype(BF)
         for a, b in plane:
             p_copy(i, a, b).start()
 
@@ -331,21 +316,13 @@
     slot_of = lax.rem(at, half) * 4 + lax.div(at, half)
     moved_t = (slot_of == source[0]).astype(F32).astype(BF)
 
-    near, far = [], []
+    pieces = []
     for i in range(CHUNKS):
-        even = psend[i, pl.ds(pl.multiple_of(rep * vis + sec * half, half), half), :].astype(F32)
-        odd = jnp.zeros_like(even)
+        mine = psend[i, pl.ds(pl.multiple_of(rep * vis + sec * half, half), half), :].astype(F32)
         for a, b in plane:
             p_copy(i, a, b).wait_recv()
-            if b % 2:
-                odd = odd + precv[i, a, b].astype(F32)
-            else:
-                even = even + precv[i, a, b].astype(F32)
-        near.append(even)
-        far.append(odd)
-    first = [jnp.where(core == 0, x, y) for x, y in zip(near, far)]
-    second = [jnp.where(core == 0, y, x) for x, y in zip(near, far)]
-    pieces = first + second
+            mine = mine + precv[i, a, b].astype(F32)
+        pieces.append(mine)
     merged = jnp.concatenate(pieces, axis=0).astype(BF)
     patch_out[0] = dot(moved_t, merged, (0, 0)).astype(BF)
 
@@ -358,8 +335,6 @@
     for a, b in across:
         sel_copy(gqsel, a_send, a_recv, a, b).wait_send()
         pass_copy(a, b).wait_send()
-    weight_copy().wait_send()
-    grad_copy().wait_send()
     for a, b in plane:
         sel_copy(kvsel, b_send, b_recv, a, b).wait_send()
         for i in range(CHUNKS):
@@ -383,7 +358,7 @@
         anywhere = pl.BlockSpec(memory_space=pl.ANY)
         inside = pl.BlockSpec(memory_space=pltpu.VMEM)
         dma = pltpu.SemaphoreType.DMA
-        model, side = wp.shape[0], wp.shape[1] // 2
+        model, side = wp.shape[0], wp.shape[1]
         shapes = (
             jax.ShapeDtypeStruct(k.shape, BF),
             jax.ShapeDtypeStruct(v.shape, BF),
@@ -413,13 +388,11 @@
                 pltpu.VMEM((n, vis, 2 * HEAD), BF),
                 pltpu.VMEM((model, wq.shape[0]), BF),
                 pltpu.VMEM((model, side), BF),
-                pltpu.VMEM((model, side), BF),
                 pltpu.VMEM((1, width), F32),
                 pltpu.VMEM((1, width), F32),
                 pltpu.VMEM((HEAD, width), F32),
                 pltpu.VMEM((sections, replicas * vis, width), BF),
                 pltpu.VMEM((sections, replicas * vis, 2 * HEAD), BF),
-                pltpu.VMEM((2, model, replicas * vis), BF),
                 pltpu.VMEM((CHUNKS, replicas * vis, side // CHUNKS), BF),
                 pltpu.VMEM((CHUNKS, sections, replicas, half, side // CHUNKS), BF),
                 dma((8 + 2 * GROUP,)),
@@ -427,7 +400,6 @@
                 dma((sections, replicas)), dma((sections, replicas)),
                 dma((sections, replicas)), dma((sections, replicas)),
                 dma((CHUNKS, sections, replicas)), dma((CHUNKS, sections, replicas)),
-                dma((1,)), dma((1,)), dma((1,)), dma((1,)),
                 dma((n,)), dma((n,)), dma((n,)), dma((n,)),
             ],
             compiler_params=pltpu.CompilerParams(

time: 34.7 us -> 37.3 us (1.075)
  Pallas kernels: 33.9 us -> 36.5 us
    pallas_call x1, Pallas kernels: 32.3 us -> 34.9 us  [shards(): pl.pallas_call(functools.partial(kernel, n, sections, replicas), out_shap...]
where the time goes in v5:
time: 37.3 us; the launch traced here: 37.1 us
  Pallas kernels  36.5 us (98%)
  between operations  0.64 us (2%)
    pallas_call x1, Pallas kernels, shards(): pl.pallas_call(functools.partial(kernel, n, sections, replicas), out_shap...  34.9 us
    pallas_call x1, Pallas kernels, shards(): pl.pallas_call(hand_on, out_shape=shapes, in_specs=[inside] * 3, out_spec...  1.59 us

profile of v5, /device:TPU:0, one launch (start us, length us, event | category | flops | bytes accessed | tf_op | source)
XLA Modules:
  0.0 37.1 jit_solution(8656993123517833402)
XLA Ops:
  0.6 34.9 %shard_map.121 = (bf16[1,128,128]{2,1,0:T(8,128)(2,1)}, bf16[1,128,128]{2,1,0:T(8,128)(2,1)}, bf16[1,64,640]{2,1,0:T(8,128)(2,1)}) custom-call(bf16[1,128,896]{2,1,0:T(8,128)(2,1)} %q_in.1, bf16[1,128,128]{2,1,0:T(8,128)(2,1)} %k_in.1, bf16[1,128,128]{2,1,0:T(8,128)(2,1)} %v_in.1, bf16[1,128,896]{2,1,0:T(8,128)(2,1)} %g_in.1, f32[7,1,128]{2,1,0:T(1,128)} %bitcast.3, ...), custom_call_target="tpu_custom_call" | custom-call | tf_op jit(solution)/shard_map/pallas_call | solution.py:367
  35.5 1.6 %shard_map.122 = (bf16[1,128,128]{2,1,0:T(8,128)(2,1)}, bf16[1,128,128]{2,1,0:T(8,128)(2,1)}, bf16[1,64,640]{2,1,0:T(8,128)(2,1)}) custom-call(bf16[1,128,128]{2,1,0:T(8,128)(2,1)} %get-tuple-element.6.a, bf16[1,128,128]{2,1,0:T(8,128)(2,1)} %get-tuple-element.7.b, bf16[1,64,640]{2,1,0:T(8,128)(2,1)} %get-tuple-element.8.c), custom_call_target="tpu_custom_call" | custom-call | tf_op jit(solution)/shard_map/pallas_call | solution.py:409

commit v6 on v4

--- a/solution.py
+++ b/solution.py
@@ -125,11 +125,6 @@
     def r_copy(o):
         return remote(rsend.at[o], rrecv.at[o], r_send.at[o], r_recv.at[o], behind(o))
 
-    def pass_copy(a, b):
-        at = pl.ds(pl.multiple_of(lax.rem(rep - b + replicas, replicas) * vis, vis), vis)
-        return remote(gqsel.at[a, at], gqsel.at[a, at], a_send.at[a, b + 1], a_recv.at[a, b + 1], partner)
-
-    across = [(a, b) for a, b in plane if b % 2 == 0]
     mine_at = pl.ds(pl.multiple_of(rep * vis, vis), vis)
 
     def sel_copy(buf, send, recv, a, b):
@@ -259,9 +254,8 @@
         gqsel[0, mine_at, h * HEAD : (h + 1) * HEAD] = dot(
             hot, gq[:, h * HEAD : (h + 1) * HEAD], (1, 1)
         ).astype(BF)
-    for a, b in across:
+    for a, b in plane:
         sel_copy(gqsel, a_send, a_recv, a, b).start()
-    pass_copy(0, 0).start()
     each(1, n, lambda o: g_copy(o).start())
 
     def picked(x):
@@ -289,15 +283,12 @@
     kvsel[0, mine_at, HEAD : 2 * HEAD] = rows_v.astype(BF)
     for a, b in plane:
         sel_copy(kvsel, b_send, b_recv, a, b).start()
-    for a, b in across:
-        sel_copy(gqsel, a_send, a_recv, a, b).wait_recv()
-        pass_copy(a, b).start()
 
     loads[2].wait()
     loads[3].wait()
     part = width + 2 * HEAD
-    for a, b in [(0, 0)] + across:
-        pass_copy(a, b).wait_recv()
+    for a, b in plane:
+        sel_copy(gqsel, a_send, a_recv, a, b).wait_recv()
 
     def weight_rows(a, offset, size):
         first = lax.rem(sec - a + sections, sections) * part + offset
@@ -354,10 +345,8 @@
     each(1, n, lambda o: g_copy(o).wait_send())
     each(1, n, lambda o: h_copy(o).wait_send())
     each(1, n, lambda o: r_copy(o).wait_send())
-    pass_copy(0, 0).wait_send()
-    for a, b in across:
+    for a, b in plane:
         sel_copy(gqsel, a_send, a_recv, a, b).wait_send()
-        pass_copy(a, b).wait_send()
     weight_copy().wait_send()
     grad_copy().wait_send()
     for a, b in plane:

time: 34.7 us -> 35.7 us (1.029)
  Pallas kernels: 33.9 us -> 34.9 us
    pallas_call x1, Pallas kernels: 32.3 us -> 33.3 us  [shards(): pl.pallas_call(functools.partial(kernel, n, sections, replicas), out_shap...]
where the time goes in v6:
time: 35.7 us; the launch traced here: 35.6 us
  Pallas kernels  34.9 us (98%)
  between operations  0.64 us (2%)
    pallas_call x1, Pallas kernels, shards(): pl.pallas_call(functools.partial(kernel, n, sections, replicas), out_shap...  33.3 us
    pallas_call x1, Pallas kernels, shards(): pl.pallas_call(hand_on, out_shape=shapes, in_specs=[inside] * 3, out_spec...  1.59 us

profile of v6, /device:TPU:0, one launch (start us, length us, event | category | flops | bytes accessed | tf_op | source)
XLA Modules:
  0.0 35.6 jit_solution(2087158415035736241)
XLA Ops:
  0.6 33.3 %shard_map.121 = (bf16[1,128,128]{2,1,0:T(8,128)(2,1)}, bf16[1,128,128]{2,1,0:T(8,128)(2,1)}, bf16[1,64,640]{2,1,0:T(8,128)(2,1)}) custom-call(bf16[1,128,896]{2,1,0:T(8,128)(2,1)} %q_in.1, bf16[1,128,128]{2,1,0:T(8,128)(2,1)} %k_in.1, bf16[1,128,128]{2,1,0:T(8,128)(2,1)} %v_in.1, bf16[1,128,896]{2,1,0:T(8,128)(2,1)} %g_in.1, f32[7,1,128]{2,1,0:T(1,128)} %bitcast.3, ...), custom_call_target="tpu_custom_call" | custom-call | tf_op jit(solution)/shard_map/pallas_call | solution.py:381
  34.0 1.6 %shard_map.122 = (bf16[1,128,128]{2,1,0:T(8,128)(2,1)}, bf16[1,128,128]{2,1,0:T(8,128)(2,1)}, bf16[1,64,640]{2,1,0:T(8,128)(2,1)}) custom-call(bf16[1,128,128]{2,1,0:T(8,128)(2,1)} %get-tuple-element.6.a, bf16[1,128,128]{2,1,0:T(8,128)(2,1)} %get-tuple-element.7.b, bf16[1,64,640]{2,1,0:T(8,128)(2,1)} %get-tuple-element.8.c), custom_call_target="tpu_custom_call" | custom-call | tf_op jit(solution)/shard_map/pallas_call | solution.py:426

commit v7 on v4

--- a/solution.py
+++ b/solution.py
@@ -262,7 +262,6 @@
     for a, b in across:
         sel_copy(gqsel, a_send, a_recv, a, b).start()
     pass_copy(0, 0).start()
-    each(1, n, lambda o: g_copy(o).start())
 
     def picked(x):
         return lax.dot_general(
@@ -292,6 +291,7 @@
     for a, b in across:
         sel_copy(gqsel, a_send, a_recv, a, b).wait_recv()
         pass_copy(a, b).start()
+    each(1, n, lambda o: g_copy(o).start())
 
     loads[2].wait()
     loads[3].wait()

time: 34.7 us -> 34.2 us (0.986)
  Pallas kernels: 33.9 us -> 33.4 us
    pallas_call x1, Pallas kernels: 32.3 us -> 31.8 us  [shards(): pl.pallas_call(functools.partial(kernel, n, sections, replicas), out_shap...]
where the time goes in v7:
time: 34.2 us; the launch traced here: 34 us
  Pallas kernels  33.4 us (98%)
  between operations  0.64 us (2%)
    pallas_call x1, Pallas kernels, shards(): pl.pallas_call(functools.partial(kernel, n, sections, replicas), out_shap...  31.8 us
    pallas_call x1, Pallas kernels, shards(): pl.pallas_call(hand_on, out_shape=shapes, in_specs=[inside] * 3, out_spec...  1.59 us

profile of v7, /device:TPU:0, one launch (start us, length us, event | category | flops | bytes accessed | tf_op | source)
XLA Modules:
  0.0 34.0 jit_solution(7513681536642097405)
XLA Ops:
  0.6 31.8 %shard_map.121 = (bf16[1,128,128]{2,1,0:T(8,128)(2,1)}, bf16[1,128,128]{2,1,0:T(8,128)(2,1)}, bf16[1,64,640]{2,1,0:T(8,128)(2,1)}) custom-call(bf16[1,128,896]{2,1,0:T(8,128)(2,1)} %q_in.1, bf16[1,128,128]{2,1,0:T(8,128)(2,1)} %k_in.1, bf16[1,128,128]{2,1,0:T(8,128)(2,1)} %v_in.1, bf16[1,128,896]{2,1,0:T(8,128)(2,1)} %g_in.1, f32[7,1,128]{2,1,0:T(1,128)} %bitcast.3, ...), custom_call_target="tpu_custom_call" | custom-call | tf_op jit(solution)/shard_map/pallas_call | solution.py:392
  32.4 1.6 %shard_map.122 = (bf16[1,128,128]{2,1,0:T(8,128)(2,1)}, bf16[1,128,128]{2,1,0:T(8,128)(2,1)}, bf16[1,64,640]{2,1,0:T(8,128)(2,1)}) custom-call(bf16[1,128,128]{2,1,0:T(8,128)(2,1)} %get-tuple-element.6.a, bf16[1,128,128]{2,1,0:T(8,128)(2,1)} %get-tuple-element.7.b, bf16[1,64,640]{2,1,0:T(8,128)(2,1)} %get-tuple-element.8.c), custom_call_target="tpu_custom_call" | custom-call | tf_op jit(solution)/shard_map/pallas_call | solution.py:437
